TPU v7x, 128 devices: a whole 4x4x4 slice. The times are simulated.
128 devices in a mesh: lat: 8 (over y, x_lo), lon: 16 (over x_hi, z, core).
Axes of the slice: x: 4 (x_hi: 2, x_lo: 2; x = x_hi * 2 + x_lo), y: 4, z: 4, core: 2. Of those that a mesh axis runs over, the one named last changes fastest.
Arguments:
- innovation: float32 [32, 524288], P(None, ('lat', 'lon')), may hold values from -6 to 6
- jacobian: float32 [32, 4, 524288], P(None, None, ('lat', 'lon')), may hold values from -1 to 1
- channel_count: int32 [524288], P(('lat', 'lon')), may hold values from 1 to 32
- owner: int32 [524288, 1], P(('lat', 'lon')), may hold values from 0 to 127; in each aligned block of 4096 rows (0 to 4095, 4096 to 8191, ...) at most 128 rows name the same one
- footprint: int32 [8, 524288], P(None, ('lat', 'lon')), may hold values from 0 to 8191
- weight: float32 [8, 524288], P(None, ('lat', 'lon')), may hold values from 0.3 to 1
- perturbation: float32 [40, 4, 256, 4096], P(None, None, 'lat', 'lon'), may hold values from -6 to 6
- scale_first: float32 [256, 4096], P('lat', 'lon'), may hold values from 0.12 to 0.245
- scale_second: float32 [256, 4096], P('lat', 'lon'), may hold values from 0.12 to 0.245
Outputs:
- gradient: float32 [40, 4, 256, 4096], P(None, None, 'lat', 'lon')
Inputs may be any that keep to these rules, and one draw needn't show every extreme that they name: Among the 4096 observations of one device, no owner is named more than 128 times, a bound that some block reaches.
All inputs are finite; a program needn't handle non-finite values.
Results may differ from a plain program's by a relative error of at most 0.00011.
Values sent between devices are 32-bit elements; how exact they have to be, the bound alone decides.
A program may use at most 128 MiB of HBM per device.

v0:
```python
import jax
import jax.numpy as jnp
from jax import lax
from jax.sharding import PartitionSpec as P

STEPS = 3


def padded_2(array, sides, width):
    for axis, dim in sides:
        devices, length = (lax.axis_size(axis), array.shape[dim])
        up = [(i, (i + 1) % devices) for i in range(devices)]
        down = [(j, i) for i, j in up]
        last = lax.slice_in_dim(array, length - width, length, axis=dim)
        initial = lax.slice_in_dim(array, 0, width, axis=dim)
        before = lax.ppermute(last, axis, up)
        after = lax.ppermute(initial, axis, down)
        array = jnp.concatenate([before, array, after], axis=dim)
    return array


def diffusion_step(padded, kappa):
    core = padded[:, 1:-1, 1:-1]
    north = padded[:, :-2, 1:-1]
    south = padded[:, 2:, 1:-1]
    west = padded[:, 1:-1, :-2]
    east = padded[:, 1:-1, 2:]
    return core + kappa * (north + south + west + east - 4.0 * core)


def shards(
    innovation,
    jacobian,
    channel_count,
    owner,
    footprint,
    weight,
    perturbation,
    scale_first,
    scale_second,
):
    chans, obs_count = innovation.shape
    levels = jacobian.shape[1]
    spots = footprint.shape[0]
    members, _, rows, cols = perturbation.shape
    n_lat = lax.axis_size("lat")
    n_lon = lax.axis_size("lon")
    devices = n_lat * n_lon
    slots = 4 * obs_count // devices
    chan_index = lax.broadcasted_iota(jnp.int32, (chans, obs_count), 0)
    live = (chan_index < channel_count[None, :]).astype(jnp.float32)
    profile = jnp.sum(jacobian * (innovation * live)[:, None, :], axis=0)
    target = owner[:, 0]
    row_iota = lax.broadcasted_iota(jnp.int32, (obs_count, obs_count), 0)
    col_iota = lax.broadcasted_iota(jnp.int32, (obs_count, obs_count), 1)
    earlier = (target[:, None] == target[None, :]) & (col_iota < row_iota)
    rank = jnp.sum(earlier.astype(jnp.int32), axis=1)
    place = target * slots + rank
    payload = jnp.concatenate([profile, weight], axis=0)
    floats = jnp.zeros((levels + spots, devices * slots), jnp.float32).at[:, place].set(payload)
    cells = jnp.zeros((spots, devices * slots), jnp.int32).at[:, place].set(footprint)
    got_floats, got_cells = (
        lax.all_to_all(
            floats.reshape(levels + spots, devices, slots),
            ("lat", "lon"),
            split_axis=1,
            concat_axis=1,
            tiled=True,
        ),
        lax.all_to_all(
            cells.reshape(spots, devices, slots),
            ("lat", "lon"),
            split_axis=1,
            concat_axis=1,
            tiled=True,
        ),
    )
    got_floats = got_floats.reshape(levels + spots, -1)
    got_cells = got_cells.reshape(-1)
    got_profile = got_floats[:levels]
    got_weight = got_floats[levels:]
    contrib = (got_weight[None, :, :] * got_profile[:, None, :]).reshape(levels, -1)
    points = got_cells.shape[0]
    block_size = 16384
    turns = points // block_size
    cell_blocks = got_cells.reshape(turns, block_size)
    value_blocks = contrib.reshape(levels, turns, block_size).transpose(1, 0, 2)
    row_ids = lax.broadcasted_iota(jnp.int32, (rows, 1), 0)
    col_ids = lax.broadcasted_iota(jnp.int32, (1, cols), 1)

    def accumulate(total, item):
        cell_block, value_block = item
        onehot_row = (cell_block[None, :] // cols == row_ids).astype(jnp.float32)
        onehot_col = (cell_block[:, None] % cols == col_ids).astype(jnp.float32)
        weighted = (value_block[:, None, :] * onehot_row[None, :, :]).reshape(
            levels * rows, block_size
        )
        added = jnp.dot(
            weighted,
            onehot_col,
            precision=lax.Precision.HIGHEST,
            preferred_element_type=jnp.float32,
        )
        return (total + added.reshape(levels, rows, cols), None)

    adjoint, _ = lax.scan(
        accumulate, jnp.zeros((levels, rows, cols), jnp.float32), (cell_blocks, value_blocks)
    )
    field = (perturbation * adjoint[None]).reshape(members * levels, rows, cols)
    first_row = lax.axis_index("lat") * rows
    total_rows = n_lat * rows
    grid_rows = first_row - 1 + lax.broadcasted_iota(jnp.int32, (rows + 2 * 1,), 0)
    valid = (grid_rows >= 0) & (grid_rows < total_rows)
    row_mask = valid.astype(jnp.float32)[None, :, None]
    for kappa in (scale_first, scale_second):
        for step_index in range(STEPS):
            padded = padded_2(field, (("lat", 1), ("lon", 2)), 1) * row_mask
            field = diffusion_step(padded, kappa)
    return field.reshape(members, levels, rows, cols)


def solution(mesh):
    return jax.shard_map(
        shards,
        mesh=mesh,
        in_specs=(
            P(None, ("lat", "lon")),
            P(None, None, ("lat", "lon")),
            P(("lat", "lon")),
            P(("lat", "lon"), None),
            P(None, ("lat", "lon")),
            P(None, ("lat", "lon")),
            P(None, None, "lat", "lon"),
            P("lat", "lon"),
            P("lat", "lon"),
        ),
        out_specs=P(None, None, "lat", "lon"),
        check_vma=False,
    )
```

profile of v0, /device:TPU:97, one launch (start us, length us, event | category | flops | bytes accessed | tf_op | source)
XLA Modules:
  0.0 538.9 jit_solution(15069698582019920503)
XLA Ops:
  0.0 16.5 %convert_reduce_fusion = s32[4096]{0:T(1024)S(1)} fusion(s32[4096]{0:T(1024)} %bitcast.49), kind=kLoop, calls=%fused_computation.24 | loop fusion | flops 83881984 | bytes 32768 | tf_op jit(solution)/shard_map/reduce_sum | solution.py:57
  22.3 14.4 %scatter_custom_fusion = f32[12,16384]{0,1:T(8,128)} fusion(s32[4096]{0:T(1024)S(1)} %bitcast.50, f32[4096,12]{1,0:T(8,128)S(1)} %copy.49, f32[]{:T(128)} %constant.76.clone.1), kind=kCustom, calls=%fused_computation.77 | custom fusion | bytes 786436 | tf_op jit(solution)/shard_map/scatter | solution.py:60
  42.8 10.2 %all-to-all-start = ((f32[12,128,128]{2,0,1:T(8,128)}), f32[12,128,128]{2,0,1:T(8,128)S(1)}, u32[]{:S(2)}, u32[]{:S(2)}) async-start(f32[12,128,128]{2,0,1:T(8,128)} %copy.50), calls=%async_computation | async-start | bytes 2097152 | tf_op jit(solution)/shard_map/all_to_all | solution.py:63
  54.9 14.7 %scatter_custom_fusion.1 = s32[8,16384]{0,1:T(8,128)} fusion(s32[4096]{0:T(1024)S(1)} %bitcast.51, s32[4096,8]{1,0:T(8,128)} %copy.51, s32[]{:T(128)} %constant.75.clone.1), kind=kCustom, calls=%fused_computation.75 | custom fusion | bytes 524800 | tf_op jit(solution)/shard_map/scatter | solution.py:61
  75.5 10.0 %all-to-all-start.1 = ((s32[8,128,128]{2,0,1:T(8,128)}), s32[8,128,128]{2,0,1:T(8,128)S(1)}, u32[]{:S(2)}, u32[]{:S(2)}) async-start(s32[8,128,128]{2,0,1:T(8,128)} %copy.52), calls=%async_computation.1 | async-start | bytes 1048576 | tf_op jit(solution)/shard_map/all_to_all | solution.py:70
  86.1 10.6 %all-to-all-done.1 = s32[8,128,128]{2,0,1:T(8,128)S(1)} async-done(((s32[8,128,128]{2,0,1:T(8,128)}), s32[8,128,128]{2,0,1:T(8,128)S(1)}, u32[]{:S(2)}, u32[]{:S(2)}) %all-to-all-start.1) | async-done | bytes 524320 | tf_op jit(solution)/shard_map/all_to_all | solution.py:70
  96.6 62.8 %while.13 = (s32[]{:T(128)}, f32[4,32,256]{2,1,0:T(8,128)S(1)}, f32[8,4,16384]{2,1,0:T(4,128)S(1)}, s32[8,16384]{1,0:T(8,128)S(1)}, s32[]{:T(128)}, /*index=5*/s32[]{:T(128)}) while((s32[]{:T(128)}, f32[4,32,256]{2,1,0:T(8,128)S(1)}, f32[8,4,16384]{2,1,0:T(4,128)S(1)}, s32[8,16384]{1,0:T(8,128)S(1)}, s32[]{:T(128)}, ...), condition=%wide.region_5.6_spmd.clone, body=%wide.region_4.5_spmd.clone.sunk | while | flops 6450282496 | bytes 22478944 | solution.py:106
  98.0 6.4 %fusion.71 = f32[4,32,256]{2,1,0:T(8,128)S(1)} fusion(s32[16384]{0:T(1024)S(1)} %add_select_fusion.2, f32[4,32,256]{2,1,0:T(8,128)S(1)} %get-tuple-element.175, pred[]{:T(512)S(6)} %compare.10, f32[4,32,16384]{2,1,0:T(8,128)S(1)} %fusion.70), kind=kOutput, calls=%fused_computation.13.clone.3 | convolution fusion | flops 6446710784 | bytes 8716289 | tf_op jit(solution)/shard_map/while/body/eval_jaxpr/dot_general | solution.py:98
  105.9 6.4 %fusion.71 = f32[4,32,256]{2,1,0:T(8,128)S(1)} fusion(s32[16384]{0:T(1024)S(1)} %add_select_fusion.2, f32[4,32,256]{2,1,0:T(8,128)S(1)} %get-tuple-element.175, pred[]{:T(512)S(6)} %compare.10, f32[4,32,16384]{2,1,0:T(8,128)S(1)} %fusion.70), kind=kOutput, calls=%fused_computation.13.clone.3 | convolution fusion | flops 6446710784 | bytes 8716289 | tf_op jit(solution)/shard_map/while/body/eval_jaxpr/dot_general | solution.py:98
  113.7 6.4 %fusion.71 = f32[4,32,256]{2,1,0:T(8,128)S(1)} fusion(s32[16384]{0:T(1024)S(1)} %add_select_fusion.2, f32[4,32,256]{2,1,0:T(8,128)S(1)} %get-tuple-element.175, pred[]{:T(512)S(6)} %compare.10, f32[4,32,16384]{2,1,0:T(8,128)S(1)} %fusion.70), kind=kOutput, calls=%fused_computation.13.clone.3 | convolution fusion | flops 6446710784 | bytes 8716289 | tf_op jit(solution)/shard_map/while/body/eval_jaxpr/dot_general | solution.py:98
  129.4 6.4 %fusion.71 = f32[4,32,256]{2,1,0:T(8,128)S(1)} fusion(s32[16384]{0:T(1024)S(1)} %add_select_fusion.2, f32[4,32,256]{2,1,0:T(8,128)S(1)} %get-tuple-element.175, pred[]{:T(512)S(6)} %compare.10, f32[4,32,16384]{2,1,0:T(8,128)S(1)} %fusion.70), kind=kOutput, calls=%fused_computation.13.clone.3 | convolution fusion | flops 6446710784 | bytes 8716289 | tf_op jit(solution)/shard_map/while/body/eval_jaxpr/dot_general | solution.py:98
  137.3 6.4 %fusion.71 = f32[4,32,256]{2,1,0:T(8,128)S(1)} fusion(s32[16384]{0:T(1024)S(1)} %add_select_fusion.2, f32[4,32,256]{2,1,0:T(8,128)S(1)} %get-tuple-element.175, pred[]{:T(512)S(6)} %compare.10, f32[4,32,16384]{2,1,0:T(8,128)S(1)} %fusion.70), kind=kOutput, calls=%fused_computation.13.clone.3 | convolution fusion | flops 6446710784 | bytes 8716289 | tf_op jit(solution)/shard_map/while/body/eval_jaxpr/dot_general | solution.py:98
  197.7 11.2 %maximum_multiply_fusion = f32[160,34,258]{2,1,0:T(8,128)} fusion(f32[160,34,1]{2,1,0:T(8,128)} %copy.56, f32[160,1,256]{2,1,0:T(1,128)} %copy-done.11, f32[160,32,256]{2,1,0:T(8,128)} %bitcast.42, f32[160,1,256]{2,1,0:T(1,128)S(1)} %collective-permute-done, f32[160,34,1]{2,1,0:T(8,128)S(1)} %copy.55, f32[34]{0:T(128)S(1)} %and_convert_fusion), kind=kLoop, calls=%fused_computation.27 | loop fusion | flops 7017600 | bytes 11228296 | tf_op jit(solution)/shard_map/mul | solution.py:117
  208.9 19.8 %fusion.36 = f32[160,32,256]{2,1,0:T(8,128)S(1)} fusion(f32[160,34,258]{2,1,0:T(8,128)} %maximum_multiply_fusion, f32[32,256]{1,0:T(8,128)S(1)} %copy-done.17), kind=kLoop, calls=%fused_computation.72 | loop fusion | flops 9175040 | bytes 31490048 | tf_op jit(solution)/shard_map/add | solution.py:28
  263.8 11.2 %maximum_multiply_fusion.1 = f32[160,34,258]{2,1,0:T(8,128)} fusion(f32[160,34,1]{2,1,0:T(8,128)} %copy.60, f32[160,1,256]{2,1,0:T(1,128)} %copy-done.13, f32[160,32,256]{2,1,0:T(8,128)} %copy-done.2, f32[160,1,256]{2,1,0:T(1,128)S(1)} %collective-permute-done.4, f32[160,34,1]{2,1,0:T(8,128)S(1)} %copy.59, f32[34]{0:T(128)S(1)} %and_convert_fusion), kind=kLoop, calls=%fused_computation.28 | loop fusion | flops 7017600 | bytes 11228296 | tf_op jit(solution)/shard_map/mul | solution.py:117
  275.0 19.8 %fusion.33 = f32[160,32,256]{2,1,0:T(8,128)S(1)} fusion(f32[160,34,258]{2,1,0:T(8,128)} %maximum_multiply_fusion.1, f32[32,256]{1,0:T(8,128)S(1)} %copy-done.17), kind=kLoop, calls=%fused_computation.66 | loop fusion | flops 9175040 | bytes 31490048 | tf_op jit(solution)/shard_map/add | solution.py:28
  324.4 11.2 %maximum_multiply_fusion.2 = f32[160,34,258]{2,1,0:T(8,128)} fusion(f32[160,34,1]{2,1,0:T(8,128)} %copy.64, f32[160,1,256]{2,1,0:T(1,128)} %copy-done.14, f32[160,32,256]{2,1,0:T(8,128)} %copy-done.3, f32[160,1,256]{2,1,0:T(1,128)S(1)} %collective-permute-done.8, f32[160,34,1]{2,1,0:T(8,128)S(1)} %copy.63, f32[34]{0:T(128)S(1)} %and_convert_fusion), kind=kLoop, calls=%fused_computation.29 | loop fusion | flops 7017600 | bytes 11228296 | tf_op jit(solution)/shard_map/mul | solution.py:117
  335.6 19.8 %fusion.30 = f32[160,32,256]{2,1,0:T(8,128)S(1)} fusion(f32[160,34,258]{2,1,0:T(8,128)} %maximum_multiply_fusion.2, f32[32,256]{1,0:T(8,128)S(1)} %copy-done.17), kind=kLoop, calls=%fused_computation.60 | loop fusion | flops 9175040 | bytes 31490048 | tf_op jit(solution)/shard_map/add | solution.py:28
  385.7 11.2 %maximum_multiply_fusion.3 = f32[160,34,258]{2,1,0:T(8,128)} fusion(f32[160,34,1]{2,1,0:T(8,128)} %copy.68, f32[160,1,256]{2,1,0:T(1,128)} %copy-done.15, f32[160,32,256]{2,1,0:T(8,128)} %copy-done.4, f32[160,1,256]{2,1,0:T(1,128)S(1)} %collective-permute-done.12, f32[160,34,1]{2,1,0:T(8,128)S(1)} %copy.67, f32[34]{0:T(128)S(1)} %and_convert_fusion), kind=kLoop, calls=%fused_computation.30 | loop fusion | flops 7017600 | bytes 11228296 | tf_op jit(solution)/shard_map/mul | solution.py:117
  396.9 19.8 %fusion.27 = f32[160,32,256]{2,1,0:T(8,128)S(1)} fusion(f32[160,34,258]{2,1,0:T(8,128)} %maximum_multiply_fusion.3, f32[32,256]{1,0:T(8,128)S(1)} %copy-done.18), kind=kLoop, calls=%fused_computation.54 | loop fusion | flops 9175040 | bytes 31490048 | tf_op jit(solution)/shard_map/add | solution.py:28
  445.8 11.2 %maximum_multiply_fusion.4 = f32[160,34,258]{2,1,0:T(8,128)} fusion(f32[160,34,1]{2,1,0:T(8,128)} %copy.72, f32[160,1,256]{2,1,0:T(1,128)} %copy-done.16, f32[160,32,256]{2,1,0:T(8,128)} %copy-done.5, f32[160,1,256]{2,1,0:T(1,128)S(1)} %collective-permute-done.16, f32[160,34,1]{2,1,0:T(8,128)S(1)} %copy.71, f32[34]{0:T(128)S(1)} %and_convert_fusion), kind=kLoop, calls=%fused_computation.31 | loop fusion | flops 7017600 | bytes 11228296 | tf_op jit(solution)/shard_map/mul | solution.py:117
  457.0 19.8 %fusion.24 = f32[160,32,256]{2,1,0:T(8,128)S(1)} fusion(f32[160,34,258]{2,1,0:T(8,128)} %maximum_multiply_fusion.4, f32[32,256]{1,0:T(8,128)S(1)} %copy-done.18), kind=kLoop, calls=%fused_computation.48 | loop fusion | flops 9175040 | bytes 31490048 | tf_op jit(solution)/shard_map/add | solution.py:28
  506.3 11.2 %maximum_multiply_fusion.5 = f32[160,34,258]{2,1,0:T(8,128)} fusion(f32[160,34,1]{2,1,0:T(8,128)} %copy.76, f32[160,1,256]{2,1,0:T(1,128)} %copy-done.12, f32[160,32,256]{2,1,0:T(8,128)} %copy-done.1, f32[160,1,256]{2,1,0:T(1,128)S(1)} %collective-permute-done.20, f32[160,34,1]{2,1,0:T(8,128)S(1)} %copy.75, f32[34]{0:T(128)S(1)} %and_convert_fusion), kind=kLoop, calls=%fused_computation.32 | loop fusion | flops 7017600 | bytes 11228296 | tf_op jit(solution)/shard_map/mul | solution.py:117
  517.5 21.2 %fusion.21 = f32[160,32,256]{2,1,0:T(8,128)} fusion(f32[160,34,258]{2,1,0:T(8,128)} %maximum_multiply_fusion.5, f32[32,256]{1,0:T(8,128)S(1)} %copy-done.18), kind=kLoop, calls=%fused_computation.42 | loop fusion | flops 9175040 | bytes 31490048 | tf_op jit(solution)/shard_map/add | solution.py:28
  (188 shorter events, 241.7 us)
Async XLA Ops:
  42.8 32.7 %all-to-all-start = ((f32[12,128,128]{2,0,1:T(8,128)}), f32[12,128,128]{2,0,1:T(8,128)S(1)}, u32[]{:S(2)}, u32[]{:S(2)}) async-start(f32[12,128,128]{2,0,1:T(8,128)} %copy.50), calls=%async_computation | async-start | bytes 2097152 | tf_op jit(solution)/shard_map/all_to_all | solution.py:63
  75.5 21.2 %all-to-all-start.1 = ((s32[8,128,128]{2,0,1:T(8,128)}), s32[8,128,128]{2,0,1:T(8,128)S(1)}, u32[]{:S(2)}, u32[]{:S(2)}) async-start(s32[8,128,128]{2,0,1:T(8,128)} %copy.52), calls=%async_computation.1 | async-start | bytes 1048576 | tf_op jit(solution)/shard_map/all_to_all | solution.py:70
  165.1 7.6 %collective-permute-start = (f32[160,1,256]{2,1,0:T(1,128)S(1)}, f32[160,1,256]{2,1,0:T(1,128)S(1)}, u32[]{:S(2)}, u32[]{:S(2)}) collective-permute-start(f32[160,1,256]{2,1,0:T(1,128)S(1)} %get-tuple-element.137), channel_id=1, source_target_pairs={{0,16},{16,32},{32,48},{48,64},{64,80},{80,96},{96,112},{112,0},{1... | collective-permute-start | bytes 491528 | tf_op jit(solution)/shard_map/ppermute | solution.py:16
  165.5 7.9 %collective-permute-start.1 = (f32[160,1,256]{2,1,0:T(1,128)S(1)}, f32[160,1,256]{2,1,0:T(1,128)S(1)}, u32[]{:S(2)}, u32[]{:S(2)}) collective-permute-start(f32[160,1,256]{2,1,0:T(1,128)S(1)} %get-tuple-element.138), channel_id=1, source_target_pairs={{16,0},{32,16},{48,32},{64,48},{80,64},{96,80},{112,96},{0,112},{1... | collective-permute-start | bytes 491528 | tf_op jit(solution)/shard_map/ppermute | solution.py:17
  185.9 9.2 %collective-permute-start.3 = (f32[160,34,1]{0,2,1:T(1,128)S(1)}, f32[160,34,1]{0,2,1:T(1,128)S(1)}, u32[]{:S(2)}, u32[]{:S(2)}) collective-permute-start(f32[160,34,1]{0,2,1:T(1,128)S(1)} %copy.54), channel_id=1, source_target_pairs={{1,0},{2,1},{3,2},{4,3},{5,4},{6,5},{7,6},{8,7},{9,8},{10,9},{11,1... | collective-permute-start | bytes 65288 | tf_op jit(solution)/shard_map/ppermute | solution.py:17
  187.4 4.9 collective-permute-start.2
  228.9 8.1 %collective-permute-start.4 = (f32[160,1,256]{2,1,0:T(1,128)S(1)}, f32[160,1,256]{2,1,0:T(1,128)S(1)}, u32[]{:S(2)}, u32[]{:S(2)}) collective-permute-start(f32[160,1,256]{2,1,0:T(1,128)S(1)} %get-tuple-element.135), channel_id=1, source_target_pairs={{0,16},{16,32},{32,48},{48,64},{64,80},{80,96},{96,112},{112,0},{1... | collective-permute-start | bytes 491528 | tf_op jit(solution)/shard_map/ppermute | solution.py:16
  229.1 8.8 %collective-permute-start.5 = (f32[160,1,256]{2,1,0:T(1,128)S(1)}, f32[160,1,256]{2,1,0:T(1,128)S(1)}, u32[]{:S(2)}, u32[]{:S(2)}) collective-permute-start(f32[160,1,256]{2,1,0:T(1,128)S(1)} %get-tuple-element.136), channel_id=1, source_target_pairs={{16,0},{32,16},{48,32},{64,48},{80,64},{96,80},{112,96},{0,112},{1... | collective-permute-start | bytes 491528 | tf_op jit(solution)/shard_map/ppermute | solution.py:17
  246.3 7.0 %collective-permute-start.6 = (f32[160,34,1]{0,2,1:T(1,128)S(1)}, f32[160,34,1]{0,2,1:T(1,128)S(1)}, u32[]{:S(2)}, u32[]{:S(2)}) collective-permute-start(f32[160,34,1]{0,2,1:T(1,128)S(1)} %copy.57), channel_id=1, source_target_pairs={{0,1},{1,2},{2,3},{3,4},{4,5},{5,6},{6,7},{7,8},{8,9},{9,10},{10,1... | collective-permute-start | bytes 65288 | tf_op jit(solution)/shard_map/ppermute | solution.py:16
  253.3 7.3 %collective-permute-start.7 = (f32[160,34,1]{0,2,1:T(1,128)}, f32[160,34,1]{0,2,1:T(1,128)}, u32[]{:S(2)}, u32[]{:S(2)}) collective-permute-start(f32[160,34,1]{0,2,1:T(1,128)} %copy.58), channel_id=1, source_target_pairs={{1,0},{2,1},{3,2},{4,3},{5,4},{6,5},{7,6},{8,7},{9,8},{10,9},{11,1... | collective-permute-start | bytes 65288 | tf_op jit(solution)/shard_map/ppermute | solution.py:17
  295.0 6.4 %collective-permute-start.8 = (f32[160,1,256]{2,1,0:T(1,128)S(1)}, f32[160,1,256]{2,1,0:T(1,128)S(1)}, u32[]{:S(2)}, u32[]{:S(2)}) collective-permute-start(f32[160,1,256]{2,1,0:T(1,128)S(1)} %get-tuple-element.133), channel_id=1, source_target_pairs={{0,16},{16,32},{32,48},{48,64},{64,80},{80,96},{96,112},{112,0},{1... | collective-permute-start | bytes 491528 | tf_op jit(solution)/shard_map/ppermute | solution.py:16
  295.5 6.4 %collective-permute-start.9 = (f32[160,1,256]{2,1,0:T(1,128)S(1)}, f32[160,1,256]{2,1,0:T(1,128)S(1)}, u32[]{:S(2)}, u32[]{:S(2)}) collective-permute-start(f32[160,1,256]{2,1,0:T(1,128)S(1)} %get-tuple-element.134), channel_id=1, source_target_pairs={{16,0},{32,16},{48,32},{64,48},{80,64},{96,80},{112,96},{0,112},{1... | collective-permute-start | bytes 491528 | tf_op jit(solution)/shard_map/ppermute | solution.py:17
  310.3 3.6 collective-permute-start.10
  313.9 7.3 %collective-permute-start.11 = (f32[160,34,1]{0,2,1:T(1,128)}, f32[160,34,1]{0,2,1:T(1,128)}, u32[]{:S(2)}, u32[]{:S(2)}) collective-permute-start(f32[160,34,1]{0,2,1:T(1,128)} %copy.62), channel_id=1, source_target_pairs={{1,0},{2,1},{3,2},{4,3},{5,4},{6,5},{7,6},{8,7},{9,8},{10,9},{11,1... | collective-permute-start | bytes 65288 | tf_op jit(solution)/shard_map/ppermute | solution.py:17
  355.6 6.3 %collective-permute-start.12 = (f32[160,1,256]{2,1,0:T(1,128)S(1)}, f32[160,1,256]{2,1,0:T(1,128)S(1)}, u32[]{:S(2)}, u32[]{:S(2)}) collective-permute-start(f32[160,1,256]{2,1,0:T(1,128)S(1)} %get-tuple-element.131), channel_id=1, source_target_pairs={{0,16},{16,32},{32,48},{48,64},{64,80},{80,96},{96,112},{112,0},{1... | collective-permute-start | bytes 491528 | tf_op jit(solution)/shard_map/ppermute | solution.py:16
  356.4 7.1 %collective-permute-start.13 = (f32[160,1,256]{2,1,0:T(1,128)S(1)}, f32[160,1,256]{2,1,0:T(1,128)S(1)}, u32[]{:S(2)}, u32[]{:S(2)}) collective-permute-start(f32[160,1,256]{2,1,0:T(1,128)S(1)} %get-tuple-element.132), channel_id=1, source_target_pairs={{16,0},{32,16},{48,32},{64,48},{80,64},{96,80},{112,96},{0,112},{1... | collective-permute-start | bytes 491528 | tf_op jit(solution)/shard_map/ppermute | solution.py:17
  375.3 7.1 %collective-permute-start.15 = (f32[160,34,1]{0,2,1:T(1,128)S(1)}, f32[160,34,1]{0,2,1:T(1,128)}, u32[]{:S(2)}, u32[]{:S(2)}) collective-permute-start(f32[160,34,1]{0,2,1:T(1,128)S(1)} %copy.66), channel_id=1, source_target_pairs={{1,0},{2,1},{3,2},{4,3},{5,4},{6,5},{7,6},{8,7},{9,8},{10,9},{11,1... | collective-permute-start | bytes 65288 | tf_op jit(solution)/shard_map/ppermute | solution.py:17
  416.9 6.3 %collective-permute-start.16 = (f32[160,1,256]{2,1,0:T(1,128)S(1)}, f32[160,1,256]{2,1,0:T(1,128)S(1)}, u32[]{:S(2)}, u32[]{:S(2)}) collective-permute-start(f32[160,1,256]{2,1,0:T(1,128)S(1)} %get-tuple-element.129), channel_id=1, source_target_pairs={{0,16},{16,32},{32,48},{48,64},{64,80},{80,96},{96,112},{112,0},{1... | collective-permute-start | bytes 491528 | tf_op jit(solution)/shard_map/ppermute | solution.py:16
  417.7 5.6 %collective-permute-start.17 = (f32[160,1,256]{2,1,0:T(1,128)S(1)}, f32[160,1,256]{2,1,0:T(1,128)S(1)}, u32[]{:S(2)}, u32[]{:S(2)}) collective-permute-start(f32[160,1,256]{2,1,0:T(1,128)S(1)} %get-tuple-element.130), channel_id=1, source_target_pairs={{16,0},{32,16},{48,32},{64,48},{80,64},{96,80},{112,96},{0,112},{1... | collective-permute-start | bytes 491528 | tf_op jit(solution)/shard_map/ppermute | solution.py:17
  435.3 7.3 %collective-permute-start.19 = (f32[160,34,1]{0,2,1:T(1,128)}, f32[160,34,1]{0,2,1:T(1,128)}, u32[]{:S(2)}, u32[]{:S(2)}) collective-permute-start(f32[160,34,1]{0,2,1:T(1,128)} %copy.70), channel_id=1, source_target_pairs={{1,0},{2,1},{3,2},{4,3},{5,4},{6,5},{7,6},{8,7},{9,8},{10,9},{11,1... | collective-permute-start | bytes 65288 | tf_op jit(solution)/shard_map/ppermute | solution.py:17
  477.0 6.4 %collective-permute-start.20 = (f32[160,1,256]{2,1,0:T(1,128)S(1)}, f32[160,1,256]{2,1,0:T(1,128)S(1)}, u32[]{:S(2)}, u32[]{:S(2)}) collective-permute-start(f32[160,1,256]{2,1,0:T(1,128)S(1)} %get-tuple-element.127), channel_id=1, source_target_pairs={{0,16},{16,32},{32,48},{48,64},{64,80},{80,96},{96,112},{112,0},{1... | collective-permute-start | bytes 491528 | tf_op jit(solution)/shard_map/ppermute | solution.py:16
  477.9 5.5 %collective-permute-start.21 = (f32[160,1,256]{2,1,0:T(1,128)S(1)}, f32[160,1,256]{2,1,0:T(1,128)S(1)}, u32[]{:S(2)}, u32[]{:S(2)}) collective-permute-start(f32[160,1,256]{2,1,0:T(1,128)S(1)} %get-tuple-element.128), channel_id=1, source_target_pairs={{16,0},{32,16},{48,32},{64,48},{80,64},{96,80},{112,96},{0,112},{1... | collective-permute-start | bytes 491528 | tf_op jit(solution)/shard_map/ppermute | solution.py:17
  491.8 3.9 collective-permute-start.22
  495.7 7.3 %collective-permute-start.23 = (f32[160,34,1]{0,2,1:T(1,128)}, f32[160,34,1]{0,2,1:T(1,128)}, u32[]{:S(2)}, u32[]{:S(2)}) collective-permute-start(f32[160,34,1]{0,2,1:T(1,128)} %copy.74), channel_id=1, source_target_pairs={{1,0},{2,1},{3,2},{4,3},{5,4},{6,5},{7,6},{8,7},{9,8},{10,9},{11,1... | collective-permute-start | bytes 65288 | tf_op jit(solution)/shard_map/ppermute | solution.py:17
  (22 other events, 124.9 us)
where the time goes:
time: 547 us; the launch traced here: 539 us
  other arithmetic  231 us (42%)
  local copies, waits for them, and re-layouts  135 us (25%)
  waiting for transfers between devices  60.5 us (11%)
  starting transfers between devices  59.2 us (11%)
  matrix products  51.6 us (9%)
    add x6, other arithmetic, diffusion_step(): return core + kappa * (north + south + west + east - 4.0 * core)  120 us
    mul x6, other arithmetic, shards(): padded = padded_2(field, (('lat', 1), ('lon', 2)), 1) * row_mask  67.3 us
    dot_general x8, matrix products, accumulate(): jnp.dot(weighted, onehot_col, precision=lax.Precision.HIGHEST, preferred_...  51.6 us
    slice x18, local copies, waits for them, and re-layouts, padded_2(): last = lax.slice_in_dim(array, length - width, length, axis=dim)  44.4 us
    ppermute x12, waiting for transfers between devices, padded_2(): after = lax.ppermute(initial, axis, down)  31.3 us
    ppermute x12, starting transfers between devices, padded_2(): after = lax.ppermute(initial, axis, down)  21.8 us
    ppermute x6, local copies, waits for them, and re-layouts, padded_2(): after = lax.ppermute(initial, axis, down)  18.7 us
    ppermute x12, waiting for transfers between devices, padded_2(): before = lax.ppermute(last, axis, up)  18.6 us
  transfers between devices with their start and end apart: 26, of which 17 were waited for; matrix products, arithmetic and copies ran while one was open for 8% of the time, Pallas kernels for 0%

commit v1 on v0

v1 whole, which is shorter than its diff:
```python
import jax
import jax.numpy as jnp
from jax import lax
from jax.experimental import pallas as pl
from jax.experimental.pallas import tpu as pltpu
from jax.sharding import PartitionSpec as P

STEPS = 3
HALO = 2 * STEPS
LANES = 128
SUB = 8
MESH = pl.DeviceIdType.MESH
F32 = jnp.float32
BF16 = jnp.bfloat16
I32 = jnp.int32
NT = (((1,), (1,)), ((), ()))


def iota(shape, dim):
    return lax.broadcasted_iota(I32, shape, dim)


def dot(a, b):
    return jnp.dot(a, b, preferred_element_type=F32)


def dot_nt(a, b):
    return lax.dot_general(a, b, NT, preferred_element_type=F32)


def vmem(limit, **kw):
    return pltpu.CompilerParams(vmem_limit_bytes=limit << 20, **kw)


def row_at(r, ct):
    return (r // SUB) * 16 + ct * SUB + r % SUB


def edges_kernel(p_ref, n_ref, s_ref, w_ref, e_ref):
    group = iota((SUB, LANES), 1) // SUB

    def load(r, ct):
        return p_ref[pl.ds(row_at(r, ct), SUB, stride=64), :]

    for r in range(HALO):
        for ct in range(2):
            n_ref[0, r, ct] = load(r, ct)
            s_ref[0, r, ct] = load(32 - HALO + r, ct)
    for b in range(2):
        w = jnp.zeros((SUB, LANES), F32)
        e = jnp.zeros((SUB, LANES), F32)
        for j in range(16):
            w = jnp.where(group == j, pltpu.roll(load(16 * b + j, 0), 8 * j, 1), w)
            e = jnp.where(group == j, pltpu.roll(load(16 * b + j, 1), (8 * j + 8) % LANES, 1), e)
        w_ref[0, b] = w
        e_ref[0, b] = e


def edges(view, groups):
    rows = jax.ShapeDtypeStruct((groups, HALO, 2, SUB, LANES), F32)
    cols = jax.ShapeDtypeStruct((groups, 2, SUB, LANES), F32)
    row_spec = pl.BlockSpec((1, HALO, 2, SUB, LANES), lambda g: (g, 0, 0, 0, 0))
    col_spec = pl.BlockSpec((1, 2, SUB, LANES), lambda g: (g, 0, 0, 0))
    return pl.pallas_call(
        edges_kernel,
        grid=(groups,),
        out_shape=(rows, rows, cols, cols),
        in_specs=[pl.BlockSpec((512, LANES), lambda g: (g, 0))],
        out_specs=(row_spec, row_spec, col_spec, col_spec),
        compiler_params=vmem(32),
        name="edges",
    )(view)


def pack_kernel(inn_ref, jac_ref, cc_ref, own_ref, foot_ref, wgt_ref, out_ref,
                tot_ref, acc_ref, sorted_ref, cnt_v, cnt_s, sem):
    chans, obs = inn_ref.shape
    blk = 256
    ones = jnp.ones((2 * blk, LANES), BF16)
    ones8 = jnp.ones((SUB, 2 * blk), BF16)
    tot_ref[...] = jnp.zeros_like(tot_ref)

    def count(i, row):
        own = own_ref[:, pl.ds(pl.multiple_of(i * 2 * blk, 2 * blk), 2 * blk)]
        hot = (iota((LANES, 2 * blk), 0) == own).astype(F32).astype(BF16)
        tot_ref[...] += dot(hot, ones)
        return row + dot_nt(ones8, hot)

    tot_row = lax.fori_loop(0, obs // (2 * blk), count, jnp.zeros((SUB, LANES), F32))
    upper = (iota((LANES, LANES), 0) < iota((LANES, LANES), 1)).astype(F32).astype(BF16)
    lower = (iota((LANES, LANES), 0) > iota((LANES, LANES), 1)).astype(F32).astype(BF16)
    cnt_v[0:SUB] = dot(tot_row.astype(BF16), upper).astype(I32)
    cnt_v[SUB:2 * SUB] = tot_row.astype(I32)
    to_smem = pltpu.make_async_copy(cnt_v, cnt_s, sem)
    to_smem.start()
    tot_ref[...] = dot(lower, tot_ref[...].astype(BF16))
    upper_b = (iota((blk, blk), 0) < iota((blk, blk), 1)).astype(F32).astype(BF16)
    acc_ref[...] = jnp.zeros_like(acc_ref)

    def block(i, carry):
        at = pl.ds(pl.multiple_of(i * blk, blk), blk)
        own = own_ref[:, at]
        hot = iota((LANES, blk), 0) == own
        hot_b = hot.astype(F32).astype(BF16)
        base = tot_ref[...]
        place = dot(hot_b, upper_b) + jnp.concatenate([base, base], axis=1)
        tot_ref[...] = base + dot(hot_b, ones[:blk])
        pos = jnp.sum(jnp.where(hot, place, 0.0), axis=0, keepdims=True).astype(I32)
        cc = cc_ref[:, at]
        prof = jnp.zeros((4, blk), F32)
        for c in range(chans):
            live = jnp.where(cc > c, inn_ref[c:c + 1, at], 0.0)
            prof = prof + jac_ref[c, :, at] * live
        full = jnp.concatenate([wgt_ref[:, at], foot_ref[:, at].astype(F32), prof, prof], axis=0)
        head = full.astype(BF16).astype(F32)
        both = jnp.concatenate([head, full - head], axis=0)
        hi = lax.shift_right_logical(pos, 8)
        lo = lax.bitwise_and(pos, 255)
        spread = jnp.concatenate([jnp.where(hi == h, both, 0.0) for h in range(obs // blk)], axis=0)
        hot_lo = (iota((blk, blk), 0) == lo).astype(F32).astype(BF16)
        acc_ref[...] += dot_nt(spread.astype(BF16), hot_lo)
        return carry

    lax.fori_loop(0, obs // blk, block, 0)
    for h in range(obs // blk):
        s = acc_ref[48 * h:48 * h + 24, :] + acc_ref[48 * h + 24:48 * h + 48, :]
        sorted_ref[2 * h] = s[:, :LANES]
        sorted_ref[2 * h + 1] = s[:, LANES:]
    for t in range(2):
        sorted_ref[obs // LANES + t] = jnp.zeros((24, LANES), F32)
    to_smem.wait()
    lane = iota((24, LANES), 1)

    def window(i, carry):
        for u in range(4):
            d = i * 4 + u
            first = cnt_s[0, d]
            number = cnt_s[SUB, d]
            t = lax.shift_right_logical(first, 7)
            off = lax.bitwise_and(first, 127)
            y = jnp.where(lane >= off, sorted_ref[t], sorted_ref[t + 1])
            y = pltpu.roll(y, lax.bitwise_and(LANES - off, 127), 1)
            out_ref[pl.ds(pl.multiple_of(d * 24, 8), 24), :] = jnp.where(lane < number, y, 0.0)
        return carry

    lax.fori_loop(0, LANES // 4, window, 0)


def pack(inn, jac, cc, own, foot, wgt):
    obs = inn.shape[1]
    return pl.pallas_call(
        pack_kernel,
        out_shape=jax.ShapeDtypeStruct((24 * LANES, LANES), F32),
        in_specs=[pl.BlockSpec(memory_space=pltpu.VMEM)] * 6,
        out_specs=pl.BlockSpec(memory_space=pltpu.VMEM),
        scratch_shapes=[
            pltpu.VMEM((LANES, LANES), F32),
            pltpu.VMEM((48 * (obs // 256), 256), F32),
            pltpu.VMEM((obs // LANES + 2, 24, LANES), F32),
            pltpu.VMEM((2 * SUB, LANES), I32),
            pltpu.SMEM((2 * SUB, LANES), I32),
            pltpu.SemaphoreType.DMA,
        ],
        compiler_params=vmem(40),
        name="pack",
    )(inn, jac, cc, own, foot, wgt)


DIRS = ((1, 0), (-1, 0), (0, 1), (0, -1), (1, 1), (1, -1), (-1, 1), (-1, -1))


def halo_copies(src, mid, wb, eb, send, recv, n_lat, n_lon):
    rows = src.shape[0]
    lat, lon = lax.axis_index("lat"), lax.axis_index("lon")
    copies = []
    for k, (dy, dx) in enumerate(DIRS):
        take = {1: pl.ds(rows - HALO, HALO), -1: pl.ds(0, HALO), 0: pl.ds(0, rows)}[dy]
        put = {1: pl.ds(0, HALO), -1: pl.ds(HALO + rows, HALO), 0: pl.ds(HALO, rows)}[dy]
        if dx == 0:
            s, d = src.at[take], mid.at[put]
        elif dx == 1:
            s, d = src.at[take, :, pl.ds(LANES, LANES)], wb.at[put]
        else:
            s, d = src.at[take, :, pl.ds(0, LANES)], eb.at[put]
        to = (lat + dy, lax.rem(lon + dx + n_lon, n_lon))
        copies.append(pltpu.make_async_remote_copy(
            src_ref=s, dst_ref=d, send_sem=send.at[k], recv_sem=recv.at[k],
            device_id=to, device_id_type=MESH))
    return copies


def when_lat(dy, lat, n_lat, fn):
    if dy == 0:
        fn()
    elif dy == 1:
        pl.when(lat < n_lat - 1)(fn)
    else:
        pl.when(lat > 0)(fn)


def halo_start(copies, lat, n_lat):
    for k, (dy, dx) in enumerate(DIRS):
        when_lat(dy, lat, n_lat, copies[k].start)


def halo_wait(copies, lat, n_lat):
    for k, (dy, dx) in enumerate(DIRS):
        when_lat(dy, lat, n_lat, copies[k].wait_send)
        when_lat(-dy, lat, n_lat, copies[k].wait_recv)


def halo_clear(mid, wb, eb, rows):
    for ref in (mid, wb, eb):
        for r in list(range(HALO)) + list(range(HALO + rows, 2 * HALO + rows)):
            ref[r] = jnp.zeros(ref.shape[1:], F32)


def halo_row(R, src, mid, wb, eb, rows):
    inner = src[R - HALO] if HALO <= R < HALO + rows else mid[R]
    lane = iota((4, LANES), 1)
    side = jnp.where(lane < HALO, eb[R], wb[R])
    return jnp.concatenate([inner, side], axis=1)


def route_kernel(n_lat, n_lon, s_ref, kap_ref, o_ref, kk_ref, mid, wb, eb,
                 send_sem, recv_sem, own_sem, hs, hr):
    lat, lon = lax.axis_index("lat"), lax.axis_index("lon")
    n = n_lat * n_lon
    me = lat * n_lon + lon
    rows = kap_ref.shape[0]
    halo_clear(mid, wb, eb, rows)
    bar = pltpu.get_barrier_semaphore()

    def place(k):
        t = lax.rem(me + k, n)
        return t, (lax.div(t, n_lon), lax.rem(t, n_lon))

    def signal(k, c):
        pl.semaphore_signal(bar, inc=1, device_id=place(k)[1], device_id_type=MESH)
        return c

    lax.fori_loop(1, n, signal, 0)
    own = pltpu.make_async_copy(s_ref.at[me, pl.ds(0, 5)], o_ref.at[me, pl.ds(0, 5)], own_sem)
    own.start()
    pl.semaphore_wait(bar, n - 1)
    copies = halo_copies(kap_ref, mid, wb, eb, hs, hr, n_lat, n_lon)
    halo_start(copies, lat, n_lat)

    def send(k, c):
        t, to = place(k)
        pltpu.make_async_remote_copy(
            src_ref=s_ref.at[t, pl.ds(0, 5)], dst_ref=o_ref.at[me, pl.ds(0, 5)],
            send_sem=send_sem, recv_sem=recv_sem, device_id=to, device_id_type=MESH).start()
        return c

    lax.fori_loop(1, n, send, 0)
    halo_wait(copies, lat, n_lat)
    for R in range(rows + 2 * HALO):
        x = halo_row(R, kap_ref, mid, wb, eb, rows)
        for q in range(4):
            kk_ref[q, R] = jnp.broadcast_to(x[q:q + 1], (SUB, x.shape[1]))
    own.wait()
    rest = pltpu.make_async_remote_copy(
        src_ref=s_ref.at[pl.ds(0, n - 1), pl.ds(0, 5)], dst_ref=o_ref.at[pl.ds(0, n - 1), pl.ds(0, 5)],
        send_sem=send_sem, recv_sem=recv_sem, device_id=place(1)[1], device_id_type=MESH)
    rest.wait_send()
    rest.wait_recv()


def halo_scratch(rows):
    return [
        pltpu.VMEM((rows + 2 * HALO, 4, 2 * LANES), F32),
        pltpu.VMEM((rows + 2 * HALO, 4, LANES), F32),
        pltpu.VMEM((rows + 2 * HALO, 4, LANES), F32),
    ]


def route(windows, kap, n_lat, n_lon):
    rows = kap.shape[0]
    any_spec = pl.BlockSpec(memory_space=pltpu.VMEM)
    return pl.pallas_call(
        lambda *refs: route_kernel(n_lat, n_lon, *refs),
        out_shape=(jax.ShapeDtypeStruct(windows.shape, F32),
                   jax.ShapeDtypeStruct((4, rows + 2 * HALO, SUB, 3 * LANES), F32)),
        in_specs=[any_spec, any_spec],
        out_specs=(any_spec, any_spec),
        scratch_shapes=halo_scratch(rows) + [
            pltpu.SemaphoreType.DMA, pltpu.SemaphoreType.DMA, pltpu.SemaphoreType.DMA,
            pltpu.SemaphoreType.DMA((8,)), pltpu.SemaphoreType.DMA((8,)),
        ],
        compiler_params=vmem(40, collective_id=0, has_side_effects=True),
        name="route",
    )(windows, kap)


def total_kernel(rx_ref, out_ref, buf, acc, cnt_v, cnt_s, sem):
    n = rx_ref.shape[0] // 24
    mask = jnp.concatenate(
        [rx_ref[pl.ds(24 * SUB * i, SUB, stride=24), :] for i in range(n // SUB)], axis=0)
    mask = jnp.where(mask > 0.0, 1.0, 0.0).astype(BF16)
    row = dot_nt(jnp.ones((SUB, LANES), BF16), mask)
    upper = (iota((LANES, LANES), 0) < iota((LANES, LANES), 1)).astype(F32).astype(BF16)
    cnt_v[0:SUB] = dot(row.astype(BF16), upper).astype(I32)
    cnt_v[SUB:2 * SUB] = row.astype(I32)
    to_smem = pltpu.make_async_copy(cnt_v, cnt_s, sem)
    to_smem.start()
    acc[...] = jnp.zeros_like(acc)
    to_smem.wait()
    lane = iota((24, LANES), 1)

    def append(i, cur):
        for u in range(4):
            s = i * 4 + u
            first = cnt_s[0, s]
            number = cnt_s[SUB, s]
            t = lax.shift_right_logical(first, 7)
            off = lax.bitwise_and(first, 127)
            y = pltpu.roll(rx_ref[pl.ds(pl.multiple_of(s * 24, 8), 24), :], off, 1)
            y = jnp.where(iota((24, LANES), 0) < 20, y, 0.0)
            merged = jnp.where(lane >= off, y, cur)
            buf[t] = merged
            cur = jnp.where(off + number >= LANES, jnp.where(lane < off, y, 0.0), merged)
        return cur

    cur = lax.fori_loop(0, n // 4, append, jnp.zeros((24, LANES), F32))
    points = cnt_s[0, n - 1] + cnt_s[SUB, n - 1]
    buf[lax.shift_right_logical(points, 7)] = cur
    sub = iota((SUB, LANES), 0)
    col_ids = iota((2 * LANES, LANES), 0)

    def tile(i, carry):
        w = buf[i, 0:8]
        cell = buf[i, 8:16].astype(I32)
        half = buf[i, 16:24]
        prof = half + pltpu.roll(half, 4, 0)
        cell_row = lax.shift_right_logical(cell, 8)
        cell_col = lax.bitwise_and(cell, 255)
        left, right = [], []
        for f in range(SUB):
            v = w[f:f + 1] * prof
            head = v.astype(BF16).astype(F32)
            both = jnp.where(sub < 4, head, v - head)
            r = jnp.broadcast_to(cell_row[f:f + 1], (SUB, LANES))
            left.append(jnp.concatenate(
                [jnp.where(r == k, both, 0.0) for k in range(32)], axis=0).astype(BF16))
            right.append(jnp.where(col_ids == cell_col[f:f + 1], 1.0, 0.0).astype(BF16))
        acc[...] += dot_nt(jnp.concatenate(left, axis=1), jnp.concatenate(right, axis=1))
        return carry

    lax.fori_loop(0, lax.shift_right_logical(points + 127, 7), tile, 0)
    for r in range(32):
        x = acc[SUB * r:SUB * r + SUB, :]
        out_ref[r] = (x + pltpu.roll(x, 4, 0))[0:4]


def total(rx, rows, cols):
    n = rx.shape[0] // 24
    return pl.pallas_call(
        total_kernel,
        out_shape=jax.ShapeDtypeStruct((rows, 4, cols), F32),
        in_specs=[pl.BlockSpec(memory_space=pltpu.VMEM)],
        out_specs=pl.BlockSpec(memory_space=pltpu.VMEM),
        scratch_shapes=[
            pltpu.VMEM((n + 1, 24, LANES), F32),
            pltpu.VMEM((SUB * rows, cols), F32),
            pltpu.VMEM((2 * SUB, LANES), I32),
            pltpu.SMEM((2 * SUB, LANES), I32),
            pltpu.SemaphoreType.DMA,
        ],
        compiler_params=vmem(40),
        name="total",
    )(rx)


def widen_kernel(n_lat, n_lon, a_ref, out_ref, mid, wb, eb, hs, hr):
    lat, lon = lax.axis_index("lat"), lax.axis_index("lon")
    rows = a_ref.shape[0]
    halo_clear(mid, wb, eb, rows)
    bar = pltpu.get_barrier_semaphore()
    for dy, dx in DIRS:
        def signal(dy=dy, dx=dx):
            pl.semaphore_signal(
                bar, inc=1, device_id=(lat + dy, lax.rem(lon + dx + n_lon, n_lon)),
                device_id_type=MESH)
        when_lat(dy, lat, n_lat, signal)
    pl.semaphore_wait(bar, 2 + 3 * jnp.minimum(lat, 1) + 3 * jnp.minimum(n_lat - 1 - lat, 1))
    copies = halo_copies(a_ref, mid, wb, eb, hs, hr, n_lat, n_lon)
    halo_start(copies, lat, n_lat)
    halo_wait(copies, lat, n_lat)
    for R in range(rows + 2 * HALO):
        x = halo_row(R, a_ref, mid, wb, eb, rows)
        out_ref[R] = jnp.concatenate([x, x], axis=0)


def widen(adjoint, n_lat, n_lon):
    rows = adjoint.shape[0]
    spec = pl.BlockSpec(memory_space=pltpu.VMEM)
    return pl.pallas_call(
        lambda *refs: widen_kernel(n_lat, n_lon, *refs),
        out_shape=jax.ShapeDtypeStruct((rows + 2 * HALO, SUB, 3 * LANES), F32),
        in_specs=[spec],
        out_specs=spec,
        scratch_shapes=halo_scratch(rows) + [
            pltpu.SemaphoreType.DMA((8,)), pltpu.SemaphoreType.DMA((8,))],
        compiler_params=vmem(40, collective_id=1, has_side_effects=True),
        name="widen",
    )(adjoint)


def diffuse_kernel(p_ref, nh_ref, sh_ref, pw_ref, pe_ref, cn_ref, cs_ref, adj_ref, kk_ref,
                   out_ref, x_ref):
    rows = 32
    ext = rows + 2 * HALO
    lane = iota((SUB, LANES), 1)

    def side(w, w_at, e, e_at):
        w = pltpu.roll(w, (LANES - 8 - w_at) % LANES, 1)
        e = pltpu.roll(e, (LANES - e_at) % LANES, 1)
        return jnp.where(lane < 8, e, w)

    for R in range(ext):
        r = R - HALO
        if r < 0:
            mid = [nh_ref[0, R, ct] for ct in range(2)]
            s = side(cn_ref[0], 80 + 8 * R, cn_ref[0], 16 + 8 * R)
        elif r >= rows:
            mid = [sh_ref[0, r - rows, ct] for ct in range(2)]
            s = side(cs_ref[0], 8 * (r - rows), cs_ref[0], 64 + 8 * (r - rows))
        else:
            mid = [p_ref[pl.ds(row_at(r, ct), SUB, stride=64), :] for ct in range(2)]
            s = side(pw_ref[0, r // 16], 8 * (r % 16), pe_ref[0, r // 16], 8 * (r % 16))
        x_ref[R] = jnp.concatenate(mid + [s], axis=1) * adj_ref[R]
    for step in range(1, 2 * STEPS + 1):
        q = 0 if step <= STEPS else 2
        north, center = x_ref[step - 1], x_ref[step]
        for R in range(step, ext - step):
            south = x_ref[R + 1]
            west = pltpu.roll(center, 1, 1)
            east = pltpu.roll(center, 3 * LANES - 1, 1)
            new = kk_ref[q + 1, R] * center + kk_ref[q, R] * ((north + south) + (west + east))
            if step < 2 * STEPS:
                x_ref[R] = new
            else:
                for ct in range(2):
                    out_ref[pl.ds(row_at(R - HALO, ct), SUB, stride=64), :] = (
                        new[:, ct * LANES:(ct + 1) * LANES])
            north, center = center, south


def diffuse(view, nh, sh, pw, pe, cn, cs, adj, kk):
    groups = nh.shape[0]
    row_spec = pl.BlockSpec((1, HALO, 2, SUB, LANES), lambda g: (g, 0, 0, 0, 0))
    col_spec = pl.BlockSpec((1, 2, SUB, LANES), lambda g: (g, 0, 0, 0))
    corner_spec = pl.BlockSpec((1, SUB, LANES), lambda g: (g, 0, 0))
    tile_spec = pl.BlockSpec((512, LANES), lambda g: (g, 0))
    return pl.pallas_call(
        diffuse_kernel,
        grid=(groups,),
        out_shape=jax.ShapeDtypeStruct(view.shape, F32),
        in_specs=[tile_spec, row_spec, row_spec, col_spec, col_spec, corner_spec, corner_spec,
                  pl.BlockSpec(adj.shape, lambda g: (0, 0, 0)),
                  pl.BlockSpec(kk.shape, lambda g: (0, 0, 0, 0))],
        out_specs=tile_spec,
        scratch_shapes=[pltpu.VMEM(adj.shape, F32)],
        compiler_params=vmem(48),
        name="diffuse",
    )(view, nh, sh, pw, pe, cn, cs, adj, kk)


def shards(innovation, jacobian, channel_count, owner, footprint, weight, perturbation,
           scale_first, scale_second):
    members, levels, rows, cols = perturbation.shape
    n_lat, n_lon = lax.axis_size("lat"), lax.axis_size("lon")
    fields = members * levels
    obs = innovation.shape[1]
    view = perturbation.reshape(fields, rows // SUB, SUB, cols // LANES, LANES)
    view = view.transpose(0, 1, 3, 2, 4).reshape(fields * 64, LANES)

    north, south, west, east = edges(view, fields // SUB)
    down = [(i, i + 1) for i in range(n_lat - 1)]
    up = [(i + 1, i) for i in range(n_lat - 1)]
    right = [(i, (i + 1) % n_lon) for i in range(n_lon)]
    left = [((i + 1) % n_lon, i) for i in range(n_lon)]
    pe = lax.ppermute(west, "lon", left)
    pw = lax.ppermute(east, "lon", right)
    nh = lax.ppermute(south, "lat", down)
    sh = lax.ppermute(north, "lat", up)
    lane = lax.broadcasted_iota(I32, (1, SUB, LANES), 2)
    top = jnp.where(lane < 48, pw[:, 0], jnp.roll(pe[:, 0], 64, axis=2))
    bottom = jnp.where(lane >= 80, pw[:, 1], jnp.roll(pe[:, 1], 64, axis=2))
    cs = lax.ppermute(top, "lat", up)
    cn = lax.ppermute(bottom, "lat", down)

    windows = pack(innovation, jacobian, channel_count.reshape(1, obs), owner.reshape(1, obs),
                   footprint, weight)
    kap = jnp.stack([scale_first, 1.0 - 4.0 * scale_first, scale_second, 1.0 - 4.0 * scale_second],
                    axis=1)
    n = n_lat * n_lon
    got, kk = route(windows.reshape(n, 6, 4, LANES), kap, n_lat, n_lon)
    adjoint = total(got.reshape(n * 24, LANES), rows, cols)
    adj = widen(adjoint, n_lat, n_lon)
    out = diffuse(view, nh, sh, pw, pe, cn, cs, adj, kk)
    out = out.reshape(fields, rows // SUB, cols // LANES, SUB, LANES).transpose(0, 1, 3, 2, 4)
    return out.reshape(members, levels, rows, cols)


def solution(mesh):
    both = ("lat", "lon")
    return jax.shard_map(
        shards,
        mesh=mesh,
        in_specs=(
            P(None, both),
            P(None, None, both),
            P(both),
            P(both, None),
            P(None, both),
            P(None, both),
            P(None, None, "lat", "lon"),
            P("lat", "lon"),
            P("lat", "lon"),
        ),
        out_specs=P(None, None, "lat", "lon"),
        check_vma=False,
    )
```

time: 547 us -> 175 us (0.32)
  the two profiles are of different devices: /device:TPU:97 before, /device:TPU:1 now
where the time goes in v1:
time: 175 us
  Pallas kernels  158 us (90%)
  starting transfers between devices  13.5 us (8%)
  local copies, waits for them, and re-layouts  2.79 us (2%)
    pallas_call x1, Pallas kernels, route(): pl.pallas_call(lambda *refs: route_kernel(n_lat, n_lon, *refs), out_shape...  52.6 us
    pallas_call x1, Pallas kernels, widen(): pl.pallas_call(lambda *refs: widen_kernel(n_lat, n_lon, *refs), out_shape...  45.4 us
    pallas_call x1, Pallas kernels, diffuse(): pl.pallas_call(diffuse_kernel, grid=(groups,), out_shape=jax.ShapeDtypeSt...  33.9 us
    pallas_call x1, Pallas kernels, pack(): pl.pallas_call(pack_kernel, out_shape=jax.ShapeDtypeStruct((24 * LANES, L...  12.4 us
    pallas_call x1, Pallas kernels, total(): pl.pallas_call(total_kernel, out_shape=jax.ShapeDtypeStruct((rows, 4, col...  9.18 us
    ppermute x1, starting transfers between devices, shards(): cn = lax.ppermute(bottom, 'lat', down)  4.61 us
    pallas_call x1, Pallas kernels, edges(): pl.pallas_call(edges_kernel, grid=(groups,), out_shape=(rows, rows, cols,...  4.26 us
  transfers between devices with their start and end apart: 6, of which 0 were waited for; matrix products, arithmetic and copies ran while one was open for 0% of the time, Pallas kernels for 68%

profile of v1, /device:TPU:1, one launch (start us, length us, event | category | flops | bytes accessed | tf_op | source)
XLA Modules:
  0.0 174.7 jit_solution(7930525898288318929)
XLA Ops:
  0.0 2.5 %copy-done = f32[40,4,32,256]{3,2,1,0:T(8,128)S(1)} copy-done((f32[40,4,32,256]{3,2,1,0:T(8,128)S(1)}, f32[40,4,32,256]{3,2,1,0:T(8,128)}, u32[]{:S(2)}) %copy-start) | copy-done | bytes 5242904
  2.5 0.0 copy-start.3
  2.5 4.3 %edges.1 = (f32[20,6,2,8,128]{4,3,2,1,0:T(8,128)S(1)}, f32[20,6,2,8,128]{4,3,2,1,0:T(8,128)S(1)}, f32[20,2,8,128]{3,2,1,0:T(8,128)S(1)}, f32[20,2,8,128]{3,2,1,0:T(8,128)S(1)}) custom-call(f32[10240,128]{1,0:T(8,128)S(1)} %bitcast.29), custom_call_target="tpu_custom_call" | custom-call | tf_op jit(solution)/shard_map/edges/pallas_call | solution.py:64
  6.8 1.5 collective-permute-start.3
  8.3 1.7 collective-permute-start.2
  10.0 3.2 %collective-permute-start = (f32[20,6,2,8,128]{4,3,2,1,0:T(8,128)S(1)}, f32[20,6,2,8,128]{4,3,2,1,0:T(8,128)S(1)}, u32[]{:S(2)}, u32[]{:S(2)}) collective-permute-start(f32[20,6,2,8,128]{4,3,2,1,0:T(8,128)S(1)} %get-tuple-element.11), channel_id=1, source_target_pairs={{0,16},{16,32},{32,48},{48,64},{64,80},{80,96},{96,112},{1,17},{17... | collective-permute-start | bytes 2949128 | tf_op jit(solution)/shard_map/ppermute | solution.py:486
  13.2 1.3 collective-permute-start.1
  14.5 0.0 copy-done.8
  14.7 12.4 %pack.1 = f32[3072,128]{1,0:T(8,128)S(1)} custom-call(f32[32,4096]{1,0:T(8,128)S(1)} %copy-done.2, f32[32,4,4096]{2,1,0:T(4,128)S(1)} %copy-done.1, s32[1,4096]{1,0:T(1,128)S(1)} %bitcast.32, s32[1,4096]{1,0:T(1,128)S(1)} %bitcast.33, s32[8,4096]{1,0:T(8,128)S(1)} %copy-done.3, f32[8,4096]{1,0:T(8,128)S(1)} %copy-done.4), custom_call_target="tpu_custom_call" | custom-call | tf_op jit(solution)/shard_map/pack/pallas_call | solution.py:151
  27.2 0.0 collective-permute-done.3
  27.2 0.1 fusion.2
  27.3 0.0 collective-permute-done.2
  27.3 0.1 fusion
  27.4 1.3 collective-permute-start.5
  28.7 4.6 %collective-permute-start.4 = (f32[20,8,128]{2,1,0:T(8,128)S(1)}, f32[20,8,128]{2,1,0:T(8,128)S(1)}, u32[]{:S(2)}, u32[]{:S(2)}) collective-permute-start(f32[20,8,128]{2,1,0:T(8,128)S(1)} %get-tuple-element.18), channel_id=1, source_target_pairs={{0,16},{16,32},{32,48},{48,64},{64,80},{80,96},{96,112},{1,17},{17... | collective-permute-start | bytes 245768 | tf_op jit(solution)/shard_map/ppermute | solution.py:492
  33.4 0.1 pad_maximum_fusion.refs_1_
  33.5 52.6 %route.1 = (f32[128,6,4,128]{3,2,1,0:T(4,128)S(1)}, f32[4,44,8,384]{3,2,1,0:T(8,128)S(1)}) custom-call(f32[128,6,4,128]{3,2,1,0:T(4,128)S(1)} %bitcast.30, f32[32,4,256]{2,1,0:T(4,128)S(1)} %pad_maximum_fusion.refs_1_), custom_call_target="tpu_custom_call" | custom-call | tf_op jit(solution)/shard_map/route/pallas_call | solution.py:281
  86.1 9.2 %total.1.refs_0_ = f32[32,4,256]{2,1,0:T(4,128)S(1)} custom-call(f32[3072,128]{1,0:T(8,128)S(1)} %bitcast.31), custom_call_target="tpu_custom_call" | custom-call | tf_op jit(solution)/shard_map/total/pallas_call | solution.py:358
  95.2 45.4 %widen.1.adj_ref = f32[44,8,384]{2,1,0:T(8,128)S(1)} custom-call(f32[32,4,256]{2,1,0:T(4,128)S(1)} %total.1.refs_0_), custom_call_target="tpu_custom_call" | custom-call | tf_op jit(solution)/shard_map/widen/pallas_call | solution.py:398
  140.7 0.0 collective-permute-done.5.cs_ref
  140.7 0.0 collective-permute-done.4.cn_ref
  140.7 0.0 collective-permute-done.nh_ref
  140.7 0.0 collective-permute-done.1.sh_ref
  140.8 33.9 %diffuse.1 = f32[10240,128]{1,0:T(8,128)} custom-call(f32[10240,128]{1,0:T(8,128)} %bitcast.28, f32[20,6,2,8,128]{4,3,2,1,0:T(8,128)S(1)} %collective-permute-done.nh_ref, f32[20,6,2,8,128]{4,3,2,1,0:T(8,128)S(1)} %collective-permute-done.1.sh_ref, f32[20,2,8,128]{3,2,1,0:T(8,128)S(1)} %copy.13.pw_ref, f32[20,2,8,128]{3,2,1,0:T(8,128)S(1)} %copy.14.pe_ref, ...), custom_call_target="tpu_custom_call" | custom-call | tf_op jit(solution)/shard_map/diffuse/pallas_call | solution.py:456
  (27 shorter events, 0.2 us)
Async XLA Ops:
  0.0 2.5 %copy-start = (f32[40,4,32,256]{3,2,1,0:T(8,128)S(1)}, f32[40,4,32,256]{3,2,1,0:T(8,128)}, u32[]{:S(2)}) copy-start(f32[40,4,32,256]{3,2,1,0:T(8,128)} %param.15) | copy-start | bytes 15728644
  2.5 12.0 %copy-start.7 = (f32[32,256]{1,0:T(8,128)S(1)}, f32[32,256]{1,0:T(8,128)}, u32[]{:S(2)}) copy-start(f32[32,256]{1,0:T(8,128)} %param.16) | copy-start | bytes 98308
  2.5 12.0 %copy-start.8 = (f32[32,256]{1,0:T(8,128)S(1)}, f32[32,256]{1,0:T(8,128)}, u32[]{:S(2)}) copy-start(f32[32,256]{1,0:T(8,128)} %param.17) | copy-start | bytes 98308
  2.5 12.2 %copy-start.1 = (f32[32,4,4096]{2,1,0:T(4,128)S(1)}, f32[32,4,4096]{2,1,0:T(4,128)}, u32[]{:S(2)}) copy-start(f32[32,4,4096]{2,1,0:T(4,128)} %jac_ref.1) | copy-start | bytes 6291460
  2.5 12.2 %copy-start.2 = (f32[32,4096]{1,0:T(8,128)S(1)}, f32[32,4096]{1,0:T(8,128)}, u32[]{:S(2)}) copy-start(f32[32,4096]{1,0:T(8,128)} %inn_ref.1) | copy-start | bytes 1572868
  2.5 12.2 %copy-start.3 = (s32[8,4096]{1,0:T(8,128)S(1)}, s32[8,4096]{1,0:T(8,128)}, u32[]{:S(2)}) copy-start(s32[8,4096]{1,0:T(8,128)} %foot_ref.1) | copy-start | bytes 393220
  2.5 12.2 %copy-start.4 = (f32[8,4096]{1,0:T(8,128)S(1)}, f32[8,4096]{1,0:T(8,128)}, u32[]{:S(2)}) copy-start(f32[8,4096]{1,0:T(8,128)} %wgt_ref.1) | copy-start | bytes 393220
  2.5 12.2 %copy-start.5 = (s32[4096]{0:T(1024)S(1)}, s32[4096]{0:T(1024)}, u32[]{:S(2)}) copy-start(s32[4096]{0:T(1024)} %param.11) | copy-start | bytes 49156
  2.5 12.2 %copy-start.6 = (s32[4096,1]{0,1:T(1,128)S(1)}, s32[4096,1]{0,1:T(1,128)}, u32[]{:S(2)}) copy-start(s32[4096,1]{0,1:T(1,128)} %param.12) | copy-start | bytes 49156
  6.8 20.3 %collective-permute-start.3 = (f32[20,2,8,128]{3,2,0,1:T(8,128)S(1)}, f32[20,2,8,128]{3,2,0,1:T(8,128)S(1)}, u32[]{:S(2)}, u32[]{:S(2)}) collective-permute-start(f32[20,2,8,128]{3,2,0,1:T(8,128)S(1)} %copy.11), channel_id=1, source_target_pairs={{1,0},{2,1},{3,2},{4,3},{5,4},{6,5},{7,6},{8,7},{9,8},{10,9},{11,1... | collective-permute-start | bytes 491528 | tf_op jit(solution)/shard_map/ppermute | solution.py:484
  8.3 19.0 %collective-permute-start.2 = (f32[20,2,8,128]{3,2,0,1:T(8,128)S(1)}, f32[20,2,8,128]{3,2,0,1:T(8,128)S(1)}, u32[]{:S(2)}, u32[]{:S(2)}) collective-permute-start(f32[20,2,8,128]{3,2,0,1:T(8,128)S(1)} %copy.10), channel_id=1, source_target_pairs={{0,1},{1,2},{2,3},{3,4},{4,5},{5,6},{6,7},{7,8},{8,9},{9,10},{10,1... | collective-permute-start | bytes 491528 | tf_op jit(solution)/shard_map/ppermute | solution.py:485
  10.0 130.7 %collective-permute-start = (f32[20,6,2,8,128]{4,3,2,1,0:T(8,128)S(1)}, f32[20,6,2,8,128]{4,3,2,1,0:T(8,128)S(1)}, u32[]{:S(2)}, u32[]{:S(2)}) collective-permute-start(f32[20,6,2,8,128]{4,3,2,1,0:T(8,128)S(1)} %get-tuple-element.11), channel_id=1, source_target_pairs={{0,16},{16,32},{32,48},{48,64},{64,80},{80,96},{96,112},{1,17},{17... | collective-permute-start | bytes 2949128 | tf_op jit(solution)/shard_map/ppermute | solution.py:486
  13.2 127.6 %collective-permute-start.1 = (f32[20,6,2,8,128]{4,3,2,1,0:T(8,128)S(1)}, f32[20,6,2,8,128]{4,3,2,1,0:T(8,128)S(1)}, u32[]{:S(2)}, u32[]{:S(2)}) collective-permute-start(f32[20,6,2,8,128]{4,3,2,1,0:T(8,128)S(1)} %get-tuple-element.12), channel_id=1, source_target_pairs={{16,0},{32,16},{48,32},{64,48},{80,64},{96,80},{112,96},{17,1},{33... | collective-permute-start | bytes 2949128 | tf_op jit(solution)/shard_map/ppermute | solution.py:487
  27.4 113.3 %collective-permute-start.5 = (f32[20,8,128]{2,1,0:T(8,128)S(1)}, f32[20,8,128]{2,1,0:T(8,128)S(1)}, u32[]{:S(2)}, u32[]{:S(2)}) collective-permute-start(f32[20,8,128]{2,1,0:T(8,128)S(1)} %get-tuple-element.17), channel_id=1, source_target_pairs={{16,0},{32,16},{48,32},{64,48},{80,64},{96,80},{112,96},{17,1},{33... | collective-permute-start | bytes 245768 | tf_op jit(solution)/shard_map/ppermute | solution.py:491
  28.7 112.0 %collective-permute-start.4 = (f32[20,8,128]{2,1,0:T(8,128)S(1)}, f32[20,8,128]{2,1,0:T(8,128)S(1)}, u32[]{:S(2)}, u32[]{:S(2)}) collective-permute-start(f32[20,8,128]{2,1,0:T(8,128)S(1)} %get-tuple-element.18), channel_id=1, source_target_pairs={{0,16},{16,32},{32,48},{48,64},{64,80},{80,96},{96,112},{1,17},{17... | collective-permute-start | bytes 245768 | tf_op jit(solution)/shard_map/ppermute | solution.py:492

commit v2 on v1

v2 whole, which is shorter than its diff:
```python
import jax
import jax.numpy as jnp
import numpy as np
from jax import lax
from jax.experimental import pallas as pl
from jax.experimental.pallas import tpu as pltpu
from jax.sharding import PartitionSpec as P

STEPS = 3
HALO = 2 * STEPS
LANES = 128
SUB = 8
MESH = pl.DeviceIdType.MESH
F32 = jnp.float32
BF16 = jnp.bfloat16
I32 = jnp.int32
NT = (((1,), (1,)), ((), ()))


def iota(shape, dim):
    return lax.broadcasted_iota(I32, shape, dim)


def dot(a, b):
    return jnp.dot(a, b, preferred_element_type=F32)


def dot_nt(a, b):
    return lax.dot_general(a, b, NT, preferred_element_type=F32)


def vmem(limit, **kw):
    return pltpu.CompilerParams(vmem_limit_bytes=limit << 20, **kw)


def row_at(r, ct):
    return (r // SUB) * 16 + ct * SUB + r % SUB


def edges_kernel(p_ref, n_ref, s_ref, w_ref, e_ref):
    group = iota((SUB, LANES), 1) // SUB

    def load(r, ct):
        return p_ref[pl.ds(row_at(r, ct), SUB, stride=64), :]

    for r in range(HALO):
        for ct in range(2):
            n_ref[0, r, ct] = load(r, ct)
            s_ref[0, r, ct] = load(32 - HALO + r, ct)
    for b in range(2):
        w = jnp.zeros((SUB, LANES), F32)
        e = jnp.zeros((SUB, LANES), F32)
        for j in range(16):
            w = jnp.where(group == j, pltpu.roll(load(16 * b + j, 0), 8 * j, 1), w)
            e = jnp.where(group == j, pltpu.roll(load(16 * b + j, 1), (8 * j + 8) % LANES, 1), e)
        w_ref[0, b] = w
        e_ref[0, b] = e


def edges(view, groups):
    rows = jax.ShapeDtypeStruct((groups, HALO, 2, SUB, LANES), F32)
    cols = jax.ShapeDtypeStruct((groups, 2, SUB, LANES), F32)
    row_spec = pl.BlockSpec((1, HALO, 2, SUB, LANES), lambda g: (g, 0, 0, 0, 0))
    col_spec = pl.BlockSpec((1, 2, SUB, LANES), lambda g: (g, 0, 0, 0))
    return pl.pallas_call(
        edges_kernel,
        grid=(groups,),
        out_shape=(rows, rows, cols, cols),
        in_specs=[pl.BlockSpec((512, LANES), lambda g: (g, 0))],
        out_specs=(row_spec, row_spec, col_spec, col_spec),
        compiler_params=vmem(32),
        name="edges",
    )(view)


def pack_kernel(inn_ref, jac_ref, cc_ref, own_ref, foot_ref, wgt_ref, out_ref,
                tot_ref, acc_ref, sorted_ref, cnt_v, cnt_s, sem):
    chans, obs = inn_ref.shape
    blk = 256
    ones = jnp.ones((2 * blk, LANES), BF16)
    ones8 = jnp.ones((SUB, 2 * blk), BF16)
    tot_ref[...] = jnp.zeros_like(tot_ref)

    def count(i, row):
        own = own_ref[:, pl.ds(pl.multiple_of(i * 2 * blk, 2 * blk), 2 * blk)]
        hot = (iota((LANES, 2 * blk), 0) == own).astype(F32).astype(BF16)
        tot_ref[...] += dot(hot, ones)
        return row + dot_nt(ones8, hot)

    tot_row = lax.fori_loop(0, obs // (2 * blk), count, jnp.zeros((SUB, LANES), F32))
    upper = (iota((LANES, LANES), 0) < iota((LANES, LANES), 1)).astype(F32).astype(BF16)
    lower = (iota((LANES, LANES), 0) > iota((LANES, LANES), 1)).astype(F32).astype(BF16)
    cnt_v[0:SUB] = dot(tot_row.astype(BF16), upper).astype(I32)
    cnt_v[SUB:2 * SUB] = tot_row.astype(I32)
    to_smem = pltpu.make_async_copy(cnt_v, cnt_s, sem)
    to_smem.start()
    tot_ref[...] = dot(lower, tot_ref[...].astype(BF16))
    upper_b = (iota((blk, blk), 0) < iota((blk, blk), 1)).astype(F32).astype(BF16)
    acc_ref[...] = jnp.zeros_like(acc_ref)

    def block(i, carry):
        at = pl.ds(pl.multiple_of(i * blk, blk), blk)
        own = own_ref[:, at]
        hot = iota((LANES, blk), 0) == own
        hot_b = hot.astype(F32).astype(BF16)
        base = tot_ref[...]
        place = dot(hot_b, upper_b) + jnp.concatenate([base, base], axis=1)
        tot_ref[...] = base + dot(hot_b, ones[:blk])
        pos = jnp.sum(jnp.where(hot, place, 0.0), axis=0, keepdims=True).astype(I32)
        cc = cc_ref[:, at]
        prof = jnp.zeros((4, blk), F32)
        for c in range(chans):
            live = jnp.where(cc > c, inn_ref[c:c + 1, at], 0.0)
            prof = prof + jac_ref[c, :, at] * live
        full = jnp.concatenate([wgt_ref[:, at], foot_ref[:, at].astype(F32), prof, prof], axis=0)
        head = full.astype(BF16).astype(F32)
        both = jnp.concatenate([head, full - head], axis=0)
        hi = lax.shift_right_logical(pos, 8)
        lo = lax.bitwise_and(pos, 255)
        spread = jnp.concatenate([jnp.where(hi == h, both, 0.0) for h in range(obs // blk)], axis=0)
        hot_lo = (iota((blk, blk), 0) == lo).astype(F32).astype(BF16)
        acc_ref[...] += dot_nt(spread.astype(BF16), hot_lo)
        return carry

    lax.fori_loop(0, obs // blk, block, 0)
    for h in range(obs // blk):
        s = acc_ref[48 * h:48 * h + 24, :] + acc_ref[48 * h + 24:48 * h + 48, :]
        sorted_ref[2 * h] = s[:, :LANES]
        sorted_ref[2 * h + 1] = s[:, LANES:]
    for t in range(2):
        sorted_ref[obs // LANES + t] = jnp.zeros((24, LANES), F32)
    to_smem.wait()
    lane = iota((24, LANES), 1)

    def window(i, carry):
        for u in range(4):
            d = i * 4 + u
            first = cnt_s[0, d]
            number = cnt_s[SUB, d]
            t = lax.shift_right_logical(first, 7)
            off = lax.bitwise_and(first, 127)
            y = jnp.where(lane >= off, sorted_ref[t], sorted_ref[t + 1])
            y = pltpu.roll(y, lax.bitwise_and(LANES - off, 127), 1)
            out_ref[pl.ds(pl.multiple_of(d * 24, 8), 24), :] = jnp.where(lane < number, y, 0.0)
        return carry

    lax.fori_loop(0, LANES // 4, window, 0)


def pack(inn, jac, cc, own, foot, wgt):
    obs = inn.shape[1]
    return pl.pallas_call(
        pack_kernel,
        out_shape=jax.ShapeDtypeStruct((24 * LANES, LANES), F32),
        in_specs=[pl.BlockSpec(memory_space=pltpu.VMEM)] * 6,
        out_specs=pl.BlockSpec(memory_space=pltpu.VMEM),
        scratch_shapes=[
            pltpu.VMEM((LANES, LANES), F32),
            pltpu.VMEM((48 * (obs // 256), 256), F32),
            pltpu.VMEM((obs // LANES + 2, 24, LANES), F32),
            pltpu.VMEM((2 * SUB, LANES), I32),
            pltpu.SMEM((2 * SUB, LANES), I32),
            pltpu.SemaphoreType.DMA,
        ],
        compiler_params=vmem(40),
        name="pack",
    )(inn, jac, cc, own, foot, wgt)


DIRS = ((1, 0), (-1, 0), (0, 1), (0, -1), (1, 1), (1, -1), (-1, 1), (-1, -1))


def halo_copies(src, mid, wb, eb, send, recv, n_lon):
    rows = src.shape[0]
    lat, lon = lax.axis_index("lat"), lax.axis_index("lon")
    copies = []
    for k, (dy, dx) in enumerate(DIRS):
        take = {1: pl.ds(rows - HALO, HALO), -1: pl.ds(0, HALO), 0: pl.ds(0, rows)}[dy]
        put = {1: pl.ds(0, HALO), -1: pl.ds(HALO + rows, HALO), 0: pl.ds(HALO, rows)}[dy]
        if dx == 0:
            s, d = src.at[take], mid.at[put]
        elif dx == 1:
            s, d = src.at[take, :, pl.ds(LANES, LANES)], wb.at[put]
        else:
            s, d = src.at[take, :, pl.ds(0, LANES)], eb.at[put]
        to = (lat + dy, lax.rem(lon + dx + n_lon, n_lon))
        copies.append(pltpu.make_async_remote_copy(
            src_ref=s, dst_ref=d, send_sem=send.at[k], recv_sem=recv.at[k],
            device_id=to, device_id_type=MESH))
    return copies


def when_lat(dy, lat, n_lat, fn):
    if dy == 0:
        fn()
    elif dy == 1:
        pl.when(lat < n_lat - 1)(fn)
    else:
        pl.when(lat > 0)(fn)


def halo_start(copies, lat, n_lat):
    for k, (dy, dx) in enumerate(DIRS):
        when_lat(dy, lat, n_lat, copies[k].start)


def halo_wait(copies, lat, n_lat):
    for k, (dy, dx) in enumerate(DIRS):
        when_lat(dy, lat, n_lat, copies[k].wait_send)
        when_lat(-dy, lat, n_lat, copies[k].wait_recv)


def halo_clear(mid, wb, eb, rows):
    for ref in (mid, wb, eb):
        for r in list(range(HALO)) + list(range(HALO + rows, 2 * HALO + rows)):
            ref[r] = jnp.zeros(ref.shape[1:], F32)


def lane_of(e):
    return (e % 3) * LANES + e // 3


def layouts():
    packed = np.zeros((4 * LANES, 3 * LANES), np.float32)
    whole = np.zeros((4 * LANES, 3 * LANES), np.float32)
    for c in range(2 * LANES):
        packed[c, lane_of(c + HALO)] = whole[c, lane_of(c + HALO)] = 1.0
    for q in range(LANES):
        if q % 8 >= 2:
            packed[2 * LANES + q, lane_of(q % 8 - 2)] = 1.0
        if q % 8 < HALO:
            packed[3 * LANES + q, lane_of(2 * LANES + HALO + q % 8)] = 1.0
    for q in range(HALO):
        whole[3 * LANES - HALO + q, lane_of(q)] = 1.0
        whole[3 * LANES + q, lane_of(2 * LANES + HALO + q)] = 1.0
    back = packed[:2 * LANES].T
    return [jnp.asarray(m, BF16) for m in (packed, whole, back)]


def parts(x, count):
    out = []
    for _ in range(count - 1):
        head = x.astype(BF16)
        out.append(head)
        x = x - head.astype(F32)
    return out + [x.astype(BF16)]


def moved(x, matrix, count):
    total = None
    for p in parts(x, count):
        y = dot(p, matrix)
        total = y if total is None else total + y
    return total


def interleaved(src, mid, wb, eb, whole, rows, start, count):
    lines = []
    for R in range(start, start + count):
        inner = src[R - HALO] if HALO <= R < HALO + rows else mid[R]
        lines.append(jnp.concatenate([inner, wb[R], eb[R]], axis=1))
    return moved(jnp.concatenate(lines, axis=0), whole, 3)


def route_kernel(n_lat, n_lon, s_ref, kap_ref, whole_ref, kk_ref, adj_ref,
                 got, acc, sums, mid, wb, eb, mid2, wb2, eb2,
                 send_sem, recv_sem, hs, hr, hs2, hr2):
    lat, lon = lax.axis_index("lat"), lax.axis_index("lon")
    n = n_lat * n_lon
    me = lat * n_lon + lon
    rows = kap_ref.shape[0]
    ext = rows + 2 * HALO
    groups = recv_sem.shape[0]
    per = n // groups
    halo_clear(mid, wb, eb, rows)
    halo_clear(mid2, wb2, eb2, rows)
    bar = pltpu.get_barrier_semaphore()

    def place(k):
        t = lax.rem(me + k, n)
        return t, (lax.div(t, n_lon), lax.rem(t, n_lon))

    def signal(k, c):
        pl.semaphore_signal(bar, inc=1, device_id=place(k)[1], device_id_type=MESH)
        return c

    lax.fori_loop(1, n, signal, 0)
    acc[...] = jnp.zeros_like(acc)
    pl.semaphore_wait(bar, n - 1)
    copies = halo_copies(kap_ref, mid, wb, eb, hs, hr, n_lon)
    halo_start(copies, lat, n_lat)
    for g in range(groups):
        def send(k, c, g=g):
            t, to = place(k)
            pltpu.make_async_remote_copy(
                src_ref=s_ref.at[t, pl.ds(0, 5)], dst_ref=got.at[k, pl.ds(0, 5)],
                send_sem=send_sem, recv_sem=recv_sem.at[g], device_id=to, device_id_type=MESH).start()
            return c

        lax.fori_loop(max(1, g * per), (g + 1) * per, send, 0)

    halo_wait(copies, lat, n_lat)
    for half in range(2):
        x = interleaved(kap_ref, mid, wb, eb, whole_ref[...], rows, half * ext // 2, ext // 2)
        for i in range(ext // 2):
            for q in range(4):
                line = x[4 * i + q:4 * i + q + 1]
                for t in range(3):
                    kk_ref[q, half * ext // 2 + i, t] = jnp.broadcast_to(
                        line[:, t * LANES:(t + 1) * LANES], (SUB, LANES))

    sub = iota((SUB, LANES), 0)
    row_ids = (iota((2 * LANES, LANES), 0) // SUB).astype(F32).astype(BF16)
    col_ids = iota((2 * LANES, LANES), 0).astype(F32).astype(BF16)

    def add(block):
        w = jnp.concatenate([block[0], block[1]], axis=0)
        cell = jnp.concatenate([block[2], block[3]], axis=0).astype(I32)
        prof = jnp.concatenate([block[4], block[4]], axis=0)
        cell_row = lax.shift_right_logical(cell, 8).astype(F32).astype(BF16)
        cell_col = lax.bitwise_and(cell, 255).astype(F32).astype(BF16)
        left, right = [], []
        for f in range(SUB):
            v = w[f:f + 1] * prof
            head = v.astype(BF16).astype(F32)
            both = jnp.where(sub < 4, head, v - head).astype(BF16)
            both = jnp.concatenate([both] * 32, axis=0)
            left.append(jnp.where(row_ids == cell_row[f:f + 1], both, jnp.zeros_like(both)))
            right.append(jnp.where(col_ids == cell_col[f:f + 1], jnp.ones_like(both), jnp.zeros_like(both)))
        acc[...] += dot_nt(jnp.concatenate(left, axis=1), jnp.concatenate(right, axis=1))

    add(s_ref[me])
    for g in range(groups):
        first, last = max(1, g * per), (g + 1) * per
        part = got.at[pl.ds(first, last - first), pl.ds(0, 5)]
        pltpu.make_async_remote_copy(
            src_ref=part, dst_ref=part, send_sem=send_sem, recv_sem=recv_sem.at[g],
            device_id=place(1)[1], device_id_type=MESH).wait_recv()

        def take(k, c):
            add(got[k])
            return c

        lax.fori_loop(first, last, take, 0)

    for r in range(rows):
        x = acc[SUB * r:SUB * r + SUB, :]
        sums[r] = (x + pltpu.roll(x, 4, 0))[0:4]
    copies = halo_copies(sums, mid2, wb2, eb2, hs2, hr2, n_lon)
    halo_start(copies, lat, n_lat)
    halo_wait(copies, lat, n_lat)
    x = interleaved(sums, mid2, wb2, eb2, whole_ref[...], rows, 0, ext)
    for R in range(ext):
        for t in range(3):
            v = x[4 * R:4 * R + 4, t * LANES:(t + 1) * LANES]
            adj_ref[R, t] = jnp.concatenate([v, v], axis=0)
    every = got.at[pl.ds(1, n - 1), pl.ds(0, 5)]
    pltpu.make_async_remote_copy(
        src_ref=every, dst_ref=every, send_sem=send_sem, recv_sem=recv_sem.at[0],
        device_id=place(1)[1], device_id_type=MESH).wait_send()


def route(windows, kap, whole, n_lat, n_lon):
    rows = kap.shape[0]
    ext = rows + 2 * HALO
    spec = pl.BlockSpec(memory_space=pltpu.VMEM)
    halo = [pltpu.VMEM((ext, 4, w * LANES), F32) for w in (2, 1, 1)]
    return pl.pallas_call(
        lambda *refs: route_kernel(n_lat, n_lon, *refs),
        out_shape=(jax.ShapeDtypeStruct((4, ext, 3, SUB, LANES), F32),
                   jax.ShapeDtypeStruct((ext, 3, SUB, LANES), F32)),
        in_specs=[spec] * 3,
        out_specs=(spec, spec),
        scratch_shapes=[
            pltpu.VMEM(windows.shape, F32),
            pltpu.VMEM((SUB * rows, 2 * LANES), F32),
            pltpu.VMEM((rows, 4, 2 * LANES), F32),
        ] + halo + halo + [
            pltpu.SemaphoreType.DMA, pltpu.SemaphoreType.DMA((8,)),
        ] + [pltpu.SemaphoreType.DMA((8,))] * 4,
        compiler_params=vmem(48, collective_id=0, has_side_effects=True),
        name="route",
    )(windows, kap, whole)


def diffuse_kernel(p_ref, nh_ref, sh_ref, pw_ref, pe_ref, cn_ref, cs_ref, adj_ref, kk_ref,
                   into_ref, back_ref, out_ref, x_ref):
    rows = 32
    ext = rows + 2 * HALO
    group = iota((SUB, LANES), 1) // SUB

    def lines(g, R):
        r = R - HALO
        if r < 0:
            mid = [nh_ref[g, R, ct] for ct in range(2)]
            w, w_at, e, e_at = cn_ref[g], 10 + R, cn_ref[g], 2 + R
        elif r >= rows:
            mid = [sh_ref[g, r - rows, ct] for ct in range(2)]
            w, w_at, e, e_at = cs_ref[g], r - rows, cs_ref[g], 8 + r - rows
        else:
            mid = [p_ref[pl.ds(512 * g + row_at(r, ct), SUB, stride=64), :] for ct in range(2)]
            w, w_at, e, e_at = pw_ref[g, r // 16], r % 16, pe_ref[g, r // 16], r % 16
        w = jnp.where(group == w_at, w, 0.0)
        e = jnp.where(group == e_at, e, 0.0)
        return jnp.concatenate(mid + [w, e], axis=1)

    for g in range(nh_ref.shape[0]):
        for start in range(0, ext, ext // 2):
            x = jnp.concatenate([lines(g, R) for R in range(start, start + ext // 2)], axis=0)
            x = moved(x, into_ref[...], 2)
            for i in range(ext // 2):
                for t in range(3):
                    x_ref[start + i, t] = (
                        x[SUB * i:SUB * i + SUB, t * LANES:(t + 1) * LANES] * adj_ref[start + i, t])
        for step in range(1, 2 * STEPS + 1):
            q = 0 if step <= STEPS else 2
            north = [x_ref[step - 1, t] for t in range(3)]
            center = [x_ref[step, t] for t in range(3)]
            for R in range(step, ext - step):
                south = [x_ref[R + 1, t] for t in range(3)]
                c0, c1, c2 = center
                sides = [pltpu.roll(c2, 1, 1) + c1, c0 + c2, c1 + pltpu.roll(c0, LANES - 1, 1)]
                for t in range(3):
                    x_ref[R, t] = (kk_ref[q + 1, R, t] * center[t]
                                   + kk_ref[q, R, t] * ((north[t] + south[t]) + sides[t]))
                north, center = center, south
        for start in range(0, rows, rows // 2):
            y = jnp.concatenate(
                [jnp.concatenate([x_ref[HALO + r, t] for t in range(3)], axis=1)
                 for r in range(start, start + rows // 2)], axis=0)
            y = moved(y, back_ref[...], 2)
            for i in range(rows // 2):
                for ct in range(2):
                    out_ref[pl.ds(512 * g + row_at(start + i, ct), SUB, stride=64), :] = (
                        y[SUB * i:SUB * i + SUB, ct * LANES:(ct + 1) * LANES])


def diffuse(view, nh, sh, pw, pe, cn, cs, adj, kk, into, back):
    groups = nh.shape[0]
    per = 2
    row_spec = pl.BlockSpec((per, HALO, 2, SUB, LANES), lambda g: (g, 0, 0, 0, 0))
    col_spec = pl.BlockSpec((per, 2, SUB, LANES), lambda g: (g, 0, 0, 0))
    corner_spec = pl.BlockSpec((per, SUB, LANES), lambda g: (g, 0, 0))
    tile_spec = pl.BlockSpec((per * 512, LANES), lambda g: (g, 0))
    fixed = [pl.BlockSpec(a.shape, lambda g, nd=a.ndim: (0,) * nd) for a in (adj, kk, into, back)]
    return pl.pallas_call(
        diffuse_kernel,
        grid=(groups // per,),
        out_shape=jax.ShapeDtypeStruct(view.shape, F32),
        in_specs=[tile_spec, row_spec, row_spec, col_spec, col_spec, corner_spec, corner_spec] + fixed,
        out_specs=tile_spec,
        scratch_shapes=[pltpu.VMEM(adj.shape, F32)],
        compiler_params=vmem(48),
        name="diffuse",
    )(view, nh, sh, pw, pe, cn, cs, adj, kk, into, back)


def shards(innovation, jacobian, channel_count, owner, footprint, weight, perturbation,
           scale_first, scale_second):
    members, levels, rows, cols = perturbation.shape
    n_lat, n_lon = lax.axis_size("lat"), lax.axis_size("lon")
    fields = members * levels
    obs = innovation.shape[1]
    view = perturbation.reshape(fields, rows // SUB, SUB, cols // LANES, LANES)
    view = view.transpose(0, 1, 3, 2, 4).reshape(fields * 64, LANES)

    north, south, west, east = edges(view, fields // SUB)
    down = [(i, i + 1) for i in range(n_lat - 1)]
    up = [(i + 1, i) for i in range(n_lat - 1)]
    right = [(i, (i + 1) % n_lon) for i in range(n_lon)]
    left = [((i + 1) % n_lon, i) for i in range(n_lon)]
    pe = lax.ppermute(west, "lon", left)
    pw = lax.ppermute(east, "lon", right)
    nh = lax.ppermute(south, "lat", down)
    sh = lax.ppermute(north, "lat", up)
    lane = lax.broadcasted_iota(I32, (1, SUB, LANES), 2)
    top = jnp.where(lane < 48, pw[:, 0], jnp.roll(pe[:, 0], 64, axis=2))
    bottom = jnp.where(lane >= 80, pw[:, 1], jnp.roll(pe[:, 1], 64, axis=2))
    cs = lax.ppermute(top, "lat", up)
    cn = lax.ppermute(bottom, "lat", down)

    windows = pack(innovation, jacobian, channel_count.reshape(1, obs), owner.reshape(1, obs),
                   footprint, weight)
    kap = jnp.stack([scale_first, 1.0 - 4.0 * scale_first, scale_second, 1.0 - 4.0 * scale_second],
                    axis=1)
    into, whole, back = layouts()
    kk, adj = route(windows.reshape(n_lat * n_lon, 6, 4, LANES), kap, whole, n_lat, n_lon)
    out = diffuse(view, nh, sh, pw, pe, cn, cs, adj, kk, into, back)
    out = out.reshape(fields, rows // SUB, cols // LANES, SUB, LANES).transpose(0, 1, 3, 2, 4)
    return out.reshape(members, levels, rows, cols)


def solution(mesh):
    both = ("lat", "lon")
    return jax.shard_map(
        shards,
        mesh=mesh,
        in_specs=(
            P(None, both),
            P(None, None, both),
            P(both),
            P(both, None),
            P(None, both),
            P(None, both),
            P(None, None, "lat", "lon"),
            P("lat", "lon"),
            P("lat", "lon"),
        ),
        out_specs=P(None, None, "lat", "lon"),
        check_vma=False,
    )
```

time: 175 us -> 160 us (0.914); the launches traced: 175 us -> 157 us
  Pallas kernels: 158 us -> 140 us
    pallas_call x3 -> x1, Pallas kernels: 88.5 us -> 30.1 us  [diffuse(): pl.pallas_call(diffuse_kernel, grid=(groups // per,), out_shape=jax.Shape...]
    pallas_call x1, Pallas kernels: 52.6 us -> 93.4 us  [route(): pl.pallas_call(lambda *refs: route_kernel(n_lat, n_lon, *refs), out_shape...]
  transfers between devices with their start and end apart: 6 -> 6, of which waited for: 0 -> 0; matrix products, arithmetic and copies ran while one was open for 0% -> 0% of each run, Pallas kernels for 68% -> 67%
where the time goes in v2:
time: 160 us; the launch traced here: 157 us
  Pallas kernels  140 us (88%)
  starting transfers between devices  13.6 us (8%)
  local copies, waits for them, and re-layouts  2.81 us (2%)
    pallas_call x1, Pallas kernels, route(): pl.pallas_call(lambda *refs: route_kernel(n_lat, n_lon, *refs), out_shape...  93.4 us
    pallas_call x1, Pallas kernels, diffuse(): pl.pallas_call(diffuse_kernel, grid=(groups // per,), out_shape=jax.Shape...  30.1 us
    pallas_call x1, Pallas kernels, pack(): pl.pallas_call(pack_kernel, out_shape=jax.ShapeDtypeStruct((24 * LANES, L...  12.4 us
    ppermute x1, starting transfers between devices, shards(): cn = lax.ppermute(bottom, 'lat', down)  4.63 us
    pallas_call x1, Pallas kernels, edges(): pl.pallas_call(edges_kernel, grid=(groups,), out_shape=(rows, rows, cols,...  4.26 us
  transfers between devices with their start and end apart: 6, of which 0 were waited for; matrix products, arithmetic and copies ran while one was open for 0% of the time, Pallas kernels for 67%

profile of v2, /device:TPU:1, one launch (start us, length us, event | category | flops | bytes accessed | tf_op | source)
XLA Modules:
  0.0 157.2 jit_solution(11729183823014137783)
XLA Ops:
  0.0 2.5 %copy-done = f32[40,4,32,256]{3,2,1,0:T(8,128)S(1)} copy-done((f32[40,4,32,256]{3,2,1,0:T(8,128)S(1)}, f32[40,4,32,256]{3,2,1,0:T(8,128)}, u32[]{:S(2)}) %copy-start) | copy-done | bytes 5242904
  2.5 4.3 %edges.1 = (f32[20,6,2,8,128]{4,3,2,1,0:T(8,128)S(1)}, f32[20,6,2,8,128]{4,3,2,1,0:T(8,128)S(1)}, f32[20,2,8,128]{3,2,1,0:T(8,128)S(1)}, f32[20,2,8,128]{3,2,1,0:T(8,128)S(1)}) custom-call(f32[10240,128]{1,0:T(8,128)S(1)} %bitcast.28), custom_call_target="tpu_custom_call" | custom-call | tf_op jit(solution)/shard_map/edges/pallas_call | solution.py:65
  6.8 1.5 collective-permute-start.3
  8.3 1.7 %collective-permute-start.2 = (f32[20,2,8,128]{3,2,0,1:T(8,128)S(1)}, f32[20,2,8,128]{3,2,0,1:T(8,128)S(1)}, u32[]{:S(2)}, u32[]{:S(2)}) collective-permute-start(f32[20,2,8,128]{3,2,0,1:T(8,128)S(1)} %copy.13), channel_id=1, source_target_pairs={{0,1},{1,2},{2,3},{3,4},{4,5},{5,6},{6,7},{7,8},{8,9},{9,10},{10,1... | collective-permute-start | bytes 491528 | tf_op jit(solution)/shard_map/ppermute | solution.py:473
  10.0 3.2 %collective-permute-start = (f32[20,6,2,8,128]{4,3,2,1,0:T(8,128)S(1)}, f32[20,6,2,8,128]{4,3,2,1,0:T(8,128)S(1)}, u32[]{:S(2)}, u32[]{:S(2)}) collective-permute-start(f32[20,6,2,8,128]{4,3,2,1,0:T(8,128)S(1)} %get-tuple-element.11), channel_id=1, source_target_pairs={{0,16},{16,32},{32,48},{48,64},{64,80},{80,96},{96,112},{1,17},{17... | collective-permute-start | bytes 2949128 | tf_op jit(solution)/shard_map/ppermute | solution.py:474
  13.2 1.3 collective-permute-start.1
  14.5 0.0 copy-done.11
  14.7 0.0 copy-start.3
  14.8 12.4 %pack.1 = f32[3072,128]{1,0:T(8,128)S(1)} custom-call(f32[32,4096]{1,0:T(8,128)S(1)} %copy-done.2, f32[32,4,4096]{2,1,0:T(4,128)S(1)} %copy-done.1, s32[1,4096]{1,0:T(1,128)S(1)} %bitcast.30, s32[1,4096]{1,0:T(1,128)S(1)} %bitcast.31, s32[8,4096]{1,0:T(8,128)S(1)} %copy-done.6, f32[8,4096]{1,0:T(8,128)S(1)} %copy-done.7), custom_call_target="tpu_custom_call" | custom-call | tf_op jit(solution)/shard_map/pack/pallas_call | solution.py:152
  27.2 0.0 collective-permute-done.3
  27.2 0.0 copy-start.4
  27.2 0.0 copy-start.5
  27.2 0.1 fusion.2
  27.3 0.0 collective-permute-done.2
  27.4 0.1 fusion
  27.5 1.3 collective-permute-start.5
  28.8 4.6 %collective-permute-start.4 = (f32[20,8,128]{2,1,0:T(8,128)S(1)}, f32[20,8,128]{2,1,0:T(8,128)S(1)}, u32[]{:S(2)}, u32[]{:S(2)}) collective-permute-start(f32[20,8,128]{2,1,0:T(8,128)S(1)} %get-tuple-element.18), channel_id=1, source_target_pairs={{0,16},{16,32},{32,48},{48,64},{64,80},{80,96},{96,112},{1,17},{17... | collective-permute-start | bytes 245768 | tf_op jit(solution)/shard_map/ppermute | solution.py:480
  33.4 0.1 pad_maximum_fusion.refs_1_
  33.6 93.4 %route.1 = (f32[4,44,3,8,128]{4,3,2,1,0:T(8,128)S(1)}, f32[44,3,8,128]{3,2,1,0:T(8,128)S(1)}) custom-call(f32[128,6,4,128]{3,2,1,0:T(4,128)S(1)} %bitcast.29, f32[32,4,256]{2,1,0:T(4,128)S(1)} %pad_maximum_fusion.refs_1_, bf16[512,384]{1,0:T(8,128)(2,1)S(1)} %copy-done.3), custom_call_target="tpu_custom_call" | custom-call | tf_op jit(solution)/shard_map/route/pallas_call | solution.py:368
  127.0 0.0 collective-permute-done.5.cs_ref
  127.0 0.0 collective-permute-done.4.cn_ref
  127.0 0.0 collective-permute-done.nh_ref
  127.0 0.0 collective-permute-done.1.sh_ref
  127.1 30.1 %diffuse.1 = f32[10240,128]{1,0:T(8,128)} custom-call(f32[10240,128]{1,0:T(8,128)} %bitcast.27, f32[20,6,2,8,128]{4,3,2,1,0:T(8,128)S(1)} %collective-permute-done.nh_ref, f32[20,6,2,8,128]{4,3,2,1,0:T(8,128)S(1)} %collective-permute-done.1.sh_ref, f32[20,2,8,128]{3,2,1,0:T(8,128)S(1)} %copy.16.pw_ref, f32[20,2,8,128]{3,2,1,0:T(8,128)S(1)} %copy.17.pe_ref, ...), custom_call_target="tpu_custom_call" | custom-call | tf_op jit(solution)/shard_map/diffuse/pallas_call | solution.py:446
  (31 shorter events, 0.2 us)
Async XLA Ops:
  0.0 2.5 %copy-start = (f32[40,4,32,256]{3,2,1,0:T(8,128)S(1)}, f32[40,4,32,256]{3,2,1,0:T(8,128)}, u32[]{:S(2)}) copy-start(f32[40,4,32,256]{3,2,1,0:T(8,128)} %param.18) | copy-start | bytes 15728644
  2.5 12.0 %copy-start.10 = (f32[32,256]{1,0:T(8,128)S(1)}, f32[32,256]{1,0:T(8,128)}, u32[]{:S(2)}) copy-start(f32[32,256]{1,0:T(8,128)} %param.19) | copy-start | bytes 98308
  2.5 12.0 %copy-start.11 = (f32[32,256]{1,0:T(8,128)S(1)}, f32[32,256]{1,0:T(8,128)}, u32[]{:S(2)}) copy-start(f32[32,256]{1,0:T(8,128)} %param.20) | copy-start | bytes 98308
  2.5 12.2 %copy-start.1 = (f32[32,4,4096]{2,1,0:T(4,128)S(1)}, f32[32,4,4096]{2,1,0:T(4,128)}, u32[]{:S(2)}) copy-start(f32[32,4,4096]{2,1,0:T(4,128)} %jac_ref.1) | copy-start | bytes 6291460
  2.5 12.2 %copy-start.2 = (f32[32,4096]{1,0:T(8,128)S(1)}, f32[32,4096]{1,0:T(8,128)}, u32[]{:S(2)}) copy-start(f32[32,4096]{1,0:T(8,128)} %inn_ref.1) | copy-start | bytes 1572868
  2.5 12.2 %copy-start.6 = (s32[8,4096]{1,0:T(8,128)S(1)}, s32[8,4096]{1,0:T(8,128)}, u32[]{:S(2)}) copy-start(s32[8,4096]{1,0:T(8,128)} %foot_ref.1) | copy-start | bytes 393220
  2.5 12.2 %copy-start.7 = (f32[8,4096]{1,0:T(8,128)S(1)}, f32[8,4096]{1,0:T(8,128)}, u32[]{:S(2)}) copy-start(f32[8,4096]{1,0:T(8,128)} %wgt_ref.1) | copy-start | bytes 393220
  2.5 12.2 %copy-start.8 = (s32[4096]{0:T(1024)S(1)}, s32[4096]{0:T(1024)}, u32[]{:S(2)}) copy-start(s32[4096]{0:T(1024)} %param.14) | copy-start | bytes 49156
  2.5 12.2 %copy-start.9 = (s32[4096,1]{0,1:T(1,128)S(1)}, s32[4096,1]{0,1:T(1,128)}, u32[]{:S(2)}) copy-start(s32[4096,1]{0,1:T(1,128)} %param.15) | copy-start | bytes 49156
  6.8 20.4 %collective-permute-start.3 = (f32[20,2,8,128]{3,2,0,1:T(8,128)S(1)}, f32[20,2,8,128]{3,2,0,1:T(8,128)S(1)}, u32[]{:S(2)}, u32[]{:S(2)}) collective-permute-start(f32[20,2,8,128]{3,2,0,1:T(8,128)S(1)} %copy.14), channel_id=1, source_target_pairs={{1,0},{2,1},{3,2},{4,3},{5,4},{6,5},{7,6},{8,7},{9,8},{10,9},{11,1... | collective-permute-start | bytes 491528 | tf_op jit(solution)/shard_map/ppermute | solution.py:472
  8.3 19.0 %collective-permute-start.2 = (f32[20,2,8,128]{3,2,0,1:T(8,128)S(1)}, f32[20,2,8,128]{3,2,0,1:T(8,128)S(1)}, u32[]{:S(2)}, u32[]{:S(2)}) collective-permute-start(f32[20,2,8,128]{3,2,0,1:T(8,128)S(1)} %copy.13), channel_id=1, source_target_pairs={{0,1},{1,2},{2,3},{3,4},{4,5},{5,6},{6,7},{7,8},{8,9},{9,10},{10,1... | collective-permute-start | bytes 491528 | tf_op jit(solution)/shard_map/ppermute | solution.py:473
  10.0 117.0 %collective-permute-start = (f32[20,6,2,8,128]{4,3,2,1,0:T(8,128)S(1)}, f32[20,6,2,8,128]{4,3,2,1,0:T(8,128)S(1)}, u32[]{:S(2)}, u32[]{:S(2)}) collective-permute-start(f32[20,6,2,8,128]{4,3,2,1,0:T(8,128)S(1)} %get-tuple-element.11), channel_id=1, source_target_pairs={{0,16},{16,32},{32,48},{48,64},{64,80},{80,96},{96,112},{1,17},{17... | collective-permute-start | bytes 2949128 | tf_op jit(solution)/shard_map/ppermute | solution.py:474
  13.2 113.8 %collective-permute-start.1 = (f32[20,6,2,8,128]{4,3,2,1,0:T(8,128)S(1)}, f32[20,6,2,8,128]{4,3,2,1,0:T(8,128)S(1)}, u32[]{:S(2)}, u32[]{:S(2)}) collective-permute-start(f32[20,6,2,8,128]{4,3,2,1,0:T(8,128)S(1)} %get-tuple-element.12), channel_id=1, source_target_pairs={{16,0},{32,16},{48,32},{64,48},{80,64},{96,80},{112,96},{17,1},{33... | collective-permute-start | bytes 2949128 | tf_op jit(solution)/shard_map/ppermute | solution.py:475
  14.7 18.8 %copy-start.3 = (bf16[512,384]{1,0:T(8,128)(2,1)S(1)}, bf16[512,384]{1,0:T(8,128)(2,1)}, u32[]{:S(2)}) copy-start(bf16[512,384]{1,0:T(8,128)(2,1)} %constant.15.clone.refs_2_) | copy-start | bytes 1179652
  27.2 99.8 %copy-start.4 = (bf16[512,384]{1,0:T(8,128)(2,1)S(1)}, bf16[512,384]{1,0:T(8,128)(2,1)}, u32[]{:S(2)}) copy-start(bf16[512,384]{1,0:T(8,128)(2,1)} %constant.14.clone.into_ref) | copy-start | bytes 1179652
  27.2 99.8 %copy-start.5 = (bf16[384,256]{1,0:T(8,128)(2,1)S(1)}, bf16[384,256]{1,0:T(8,128)(2,1)}, u32[]{:S(2)}) copy-start(bf16[384,256]{1,0:T(8,128)(2,1)} %constant.16.clone.back_ref) | copy-start | bytes 589828
  27.5 99.5 %collective-permute-start.5 = (f32[20,8,128]{2,1,0:T(8,128)S(1)}, f32[20,8,128]{2,1,0:T(8,128)S(1)}, u32[]{:S(2)}, u32[]{:S(2)}) collective-permute-start(f32[20,8,128]{2,1,0:T(8,128)S(1)} %get-tuple-element.17), channel_id=1, source_target_pairs={{16,0},{32,16},{48,32},{64,48},{80,64},{96,80},{112,96},{17,1},{33... | collective-permute-start | bytes 245768 | tf_op jit(solution)/shard_map/ppermute | solution.py:479
  28.8 98.3 %collective-permute-start.4 = (f32[20,8,128]{2,1,0:T(8,128)S(1)}, f32[20,8,128]{2,1,0:T(8,128)S(1)}, u32[]{:S(2)}, u32[]{:S(2)}) collective-permute-start(f32[20,8,128]{2,1,0:T(8,128)S(1)} %get-tuple-element.18), channel_id=1, source_target_pairs={{0,16},{16,32},{32,48},{48,64},{64,80},{80,96},{96,112},{1,17},{17... | collective-permute-start | bytes 245768 | tf_op jit(solution)/shard_map/ppermute | solution.py:480

commit v3 on v2

--- a/solution.py
+++ b/solution.py
@@ -35,42 +35,6 @@
 
 def row_at(r, ct):
     return (r // SUB) * 16 + ct * SUB + r % SUB
-
-
-def edges_kernel(p_ref, n_ref, s_ref, w_ref, e_ref):
-    group = iota((SUB, LANES), 1) // SUB
-
-    def load(r, ct):
-        return p_ref[pl.ds(row_at(r, ct), SUB, stride=64), :]
-
-    for r in range(HALO):
-        for ct in range(2):
-            n_ref[0, r, ct] = load(r, ct)
-            s_ref[0, r, ct] = load(32 - HALO + r, ct)
-    for b in range(2):
-        w = jnp.zeros((SUB, LANES), F32)
-        e = jnp.zeros((SUB, LANES), F32)
-        for j in range(16):
-            w = jnp.where(group == j, pltpu.roll(load(16 * b + j, 0), 8 * j, 1), w)
-            e = jnp.where(group == j, pltpu.roll(load(16 * b + j, 1), (8 * j + 8) % LANES, 1), e)
-        w_ref[0, b] = w
-        e_ref[0, b] = e
-
-
-def edges(view, groups):
-    rows = jax.ShapeDtypeStruct((groups, HALO, 2, SUB, LANES), F32)
-    cols = jax.ShapeDtypeStruct((groups, 2, SUB, LANES), F32)
-    row_spec = pl.BlockSpec((1, HALO, 2, SUB, LANES), lambda g: (g, 0, 0, 0, 0))
-    col_spec = pl.BlockSpec((1, 2, SUB, LANES), lambda g: (g, 0, 0, 0))
-    return pl.pallas_call(
-        edges_kernel,
-        grid=(groups,),
-        out_shape=(rows, rows, cols, cols),
-        in_specs=[pl.BlockSpec((512, LANES), lambda g: (g, 0))],
-        out_specs=(row_spec, row_spec, col_spec, col_spec),
-        compiler_params=vmem(32),
-        name="edges",
-    )(view)
 
 
 def pack_kernel(inn_ref, jac_ref, cc_ref, own_ref, foot_ref, wgt_ref, out_ref,
@@ -234,24 +198,17 @@
         whole[3 * LANES - HALO + q, lane_of(q)] = 1.0
         whole[3 * LANES + q, lane_of(2 * LANES + HALO + q)] = 1.0
     back = packed[:2 * LANES].T
-    return [jnp.asarray(m, BF16) for m in (packed, whole, back)]
-
-
-def parts(x, count):
-    out = []
+    return [jnp.asarray(np.concatenate([m] * count), BF16)
+            for m, count in ((whole, 3), (packed, 2), (back, 2))]
+
+
+def moved(x, matrix, count):
+    parts = []
     for _ in range(count - 1):
         head = x.astype(BF16)
-        out.append(head)
+        parts.append(head)
         x = x - head.astype(F32)
-    return out + [x.astype(BF16)]
-
-
-def moved(x, matrix, count):
-    total = None
-    for p in parts(x, count):
-        y = dot(p, matrix)
-        total = y if total is None else total + y
-    return total
+    return dot(jnp.concatenate(parts + [x.astype(BF16)], axis=1), matrix)
 
 
 def interleaved(src, mid, wb, eb, whole, rows, start, count):
@@ -262,16 +219,26 @@
     return moved(jnp.concatenate(lines, axis=0), whole, 3)
 
 
-def route_kernel(n_lat, n_lon, s_ref, kap_ref, whole_ref, kk_ref, adj_ref,
-                 got, acc, sums, mid, wb, eb, mid2, wb2, eb2,
-                 send_sem, recv_sem, hs, hr, hs2, hr2):
+CHUNK = 4
+BATCH = 8
+
+
+def whole_kernel(n_lat, n_lon, s_ref, kap_ref, p_hbm, whole_ref, into_ref, back_ref, o_hbm,
+                 pv, xi, nsend, ssend, nh, sh, wsend, esend, pw, pe, tsend, bsend, cs, cn, stage,
+                 kk, adj, got, acc, sums, mid, wb, eb, mid2, wb2, eb2,
+                 send_sem, recv_sem, hs, hr, hs2, hr2, row_s, row_r, col_s, col_r, cor_s, cor_r,
+                 in_sem, out_sem):
     lat, lon = lax.axis_index("lat"), lax.axis_index("lon")
     n = n_lat * n_lon
     me = lat * n_lon + lon
     rows = kap_ref.shape[0]
     ext = rows + 2 * HALO
+    fields8 = xi.shape[0]
+    chunks = fields8 // CHUNK
     groups = recv_sem.shape[0]
     per = n // groups
+    load = pltpu.make_async_copy(p_hbm, pv, in_sem)
+    load.start()
     halo_clear(mid, wb, eb, rows)
     halo_clear(mid2, wb2, eb2, rows)
     bar = pltpu.get_barrier_semaphore()
@@ -285,10 +252,20 @@
         return c
 
     lax.fori_loop(1, n, signal, 0)
+
+    @pl.when(lat == 0)
+    def _():
+        nh[...] = jnp.zeros_like(nh)
+        cn[...] = jnp.zeros_like(cn)
+
+    @pl.when(lat == n_lat - 1)
+    def _():
+        sh[...] = jnp.zeros_like(sh)
+        cs[...] = jnp.zeros_like(cs)
+
     acc[...] = jnp.zeros_like(acc)
     pl.semaphore_wait(bar, n - 1)
-    copies = halo_copies(kap_ref, mid, wb, eb, hs, hr, n_lon)
-    halo_start(copies, lat, n_lat)
+
     for g in range(groups):
         def send(k, c, g=g):
             t, to = place(k)
@@ -298,22 +275,103 @@
             return c
 
         lax.fori_loop(max(1, g * per), (g + 1) * per, send, 0)
-
-    halo_wait(copies, lat, n_lat)
+    kap_copies = halo_copies(kap_ref, mid, wb, eb, hs, hr, n_lon)
+    halo_start(kap_copies, lat, n_lat)
+
+    group = iota((SUB, LANES), 1) // SUB
+    load.wait()
+
+    def point(g, r, ct):
+        return pv[pl.ds(512 * g + row_at(r, ct), SUB, stride=64), :]
+
+    def edge(g, c):
+        for r in range(HALO):
+            for ct in range(2):
+                nsend[g, r, ct] = point(g, r, ct)
+                ssend[g, r, ct] = point(g, rows - HALO + r, ct)
+        for b in range(2):
+            w = jnp.zeros((SUB, LANES), F32)
+            e = jnp.zeros((SUB, LANES), F32)
+            for j in range(16):
+                w = jnp.where(group == j, pltpu.roll(point(g, 16 * b + j, 0), 8 * j, 1), w)
+                e = jnp.where(group == j, pltpu.roll(point(g, 16 * b + j, 1), (8 * j + 8) % LANES, 1), e)
+            wsend[g, b] = w
+            esend[g, b] = e
+        return c
+
+    lax.fori_loop(0, fields8, edge, 0)
+    east, west = lax.rem(lon + 1, n_lon), lax.rem(lon + n_lon - 1, n_lon)
+
+    def remote(src, dst, ss, rs, to):
+        return pltpu.make_async_remote_copy(
+            src_ref=src, dst_ref=dst, send_sem=ss, recv_sem=rs, device_id=to, device_id_type=MESH)
+
+    cols = [remote(esend, pw, col_s.at[0], col_r.at[0], (lat, east)),
+            remote(wsend, pe, col_s.at[1], col_r.at[1], (lat, west))]
+    corners = [remote(bsend, cn, cor_s.at[0], cor_r.at[0], (lat + 1, lon)),
+               remote(tsend, cs, cor_s.at[1], cor_r.at[1], (lat - 1, lon))]
+
+    def row_copies(c):
+        at = pl.ds(c * CHUNK, CHUNK)
+        return [remote(ssend.at[at], nh.at[at], row_s.at[0, c], row_r.at[0, c], (lat + 1, lon)),
+                remote(nsend.at[at], sh.at[at], row_s.at[1, c], row_r.at[1, c], (lat - 1, lon))]
+
+    def start_rows(pair):
+        pl.when(lat < n_lat - 1)(pair[0].start)
+        pl.when(lat > 0)(pair[1].start)
+
+    def wait_rows(pair):
+        pl.when(lat < n_lat - 1)(pair[0].wait_send)
+        pl.when(lat > 0)(pair[0].wait_recv)
+        pl.when(lat > 0)(pair[1].wait_send)
+        pl.when(lat < n_lat - 1)(pair[1].wait_recv)
+
+    for copy in cols:
+        copy.start()
+    start_rows(row_copies(0))
+
+    halo_wait(kap_copies, lat, n_lat)
     for half in range(2):
         x = interleaved(kap_ref, mid, wb, eb, whole_ref[...], rows, half * ext // 2, ext // 2)
         for i in range(ext // 2):
             for q in range(4):
                 line = x[4 * i + q:4 * i + q + 1]
                 for t in range(3):
-                    kk_ref[q, half * ext // 2 + i, t] = jnp.broadcast_to(
+                    kk[q, half * ext // 2 + i, t] = jnp.broadcast_to(
                         line[:, t * LANES:(t + 1) * LANES], (SUB, LANES))
+
+    for copy in cols:
+        copy.wait()
+
+    def corner(g, c):
+        tsend[g] = jnp.where(group < 6, pw[g, 0], pltpu.roll(pe[g, 0], 64, 1))
+        bsend[g] = jnp.where(group >= 10, pw[g, 1], pltpu.roll(pe[g, 1], 64, 1))
+        return c
+
+    lax.fori_loop(0, fields8, corner, 0)
+    start_rows(corners)
+
+    def one(mid_rows, w, w_at, e, e_at):
+        return jnp.concatenate(
+            mid_rows + [jnp.where(group == w_at, w, 0.0), jnp.where(group == e_at, e, 0.0)], axis=1)
+
+    def inner(g, c):
+        x = jnp.concatenate(
+            [one([point(g, r, 0), point(g, r, 1)], pw[g, r // 16], r % 16, pe[g, r // 16], r % 16)
+             for r in range(rows)], axis=0)
+        x = moved(x, into_ref[...], 2)
+        for r in range(rows):
+            for t in range(3):
+                xi[g, HALO + r, t] = x[SUB * r:SUB * r + SUB, t * LANES:(t + 1) * LANES]
+        return c
+
+    lax.fori_loop(0, fields8, inner, 0)
 
     sub = iota((SUB, LANES), 0)
     row_ids = (iota((2 * LANES, LANES), 0) // SUB).astype(F32).astype(BF16)
     col_ids = iota((2 * LANES, LANES), 0).astype(F32).astype(BF16)
 
-    def add(block):
+    def spread(block):
         w = jnp.concatenate([block[0], block[1]], axis=0)
         cell = jnp.concatenate([block[2], block[3]], axis=0).astype(I32)
         prof = jnp.concatenate([block[4], block[4]], axis=0)
@@ -327,21 +385,27 @@
             both = jnp.concatenate([both] * 32, axis=0)
             left.append(jnp.where(row_ids == cell_row[f:f + 1], both, jnp.zeros_like(both)))
             right.append(jnp.where(col_ids == cell_col[f:f + 1], jnp.ones_like(both), jnp.zeros_like(both)))
+        return left, right
+
+    got[0] = s_ref[me]
+
+    def add(i, c):
+        left, right = [], []
+        for u in range(BATCH):
+            a, b = spread(got[i * BATCH + u])
+            left += a
+            right += b
         acc[...] += dot_nt(jnp.concatenate(left, axis=1), jnp.concatenate(right, axis=1))
-
-    add(s_ref[me])
+        return c
+
+    when_sent = {2: [1], 4: [2], 6: [3, 4]}
     for g in range(groups):
         first, last = max(1, g * per), (g + 1) * per
         part = got.at[pl.ds(first, last - first), pl.ds(0, 5)]
-        pltpu.make_async_remote_copy(
-            src_ref=part, dst_ref=part, send_sem=send_sem, recv_sem=recv_sem.at[g],
-            device_id=place(1)[1], device_id_type=MESH).wait_recv()
-
-        def take(k, c):
-            add(got[k])
-            return c
-
-        lax.fori_loop(first, last, take, 0)
+        remote(part, part, send_sem, recv_sem.at[g], place(1)[1]).wait_recv()
+        for c in when_sent.get(g, []):
+            start_rows(row_copies(c))
+        lax.fori_loop(g * per // BATCH, (g + 1) * per // BATCH, add, 0)
 
     for r in range(rows):
         x = acc[SUB * r:SUB * r + SUB, :]
@@ -353,106 +417,93 @@
     for R in range(ext):
         for t in range(3):
             v = x[4 * R:4 * R + 4, t * LANES:(t + 1) * LANES]
-            adj_ref[R, t] = jnp.concatenate([v, v], axis=0)
+            adj[R, t] = jnp.concatenate([v, v], axis=0)
+
+    wait_rows(corners)
+
+    def out_copy(g):
+        slot = lax.rem(g, 2)
+        return pltpu.make_async_copy(
+            stage.at[slot], o_hbm.at[pl.ds(512 * g, 512)], out_sem.at[slot])
+
+    def diffuse(g, c):
+        lines = [one([nh[g, j, 0], nh[g, j, 1]], cn[g], 10 + j, cn[g], 2 + j) for j in range(HALO)]
+        lines += [one([sh[g, j, 0], sh[g, j, 1]], cs[g], j, cs[g], 8 + j) for j in range(HALO)]
+        x = moved(jnp.concatenate(lines, axis=0), into_ref[...], 2)
+        for j in range(2 * HALO):
+            R = j if j < HALO else rows + j
+            for t in range(3):
+                xi[g, R, t] = x[SUB * j:SUB * j + SUB, t * LANES:(t + 1) * LANES] * adj[R, t]
+        for R in range(HALO, HALO + rows):
+            for t in range(3):
+                xi[g, R, t] = xi[g, R, t] * adj[R, t]
+        for step in range(1, 2 * STEPS + 1):
+            q = 0 if step <= STEPS else 2
+            north = [xi[g, step - 1, t] for t in range(3)]
+            center = [xi[g, step, t] for t in range(3)]
+            for R in range(step, ext - step):
+                south = [xi[g, R + 1, t] for t in range(3)]
+                c0, c1, c2 = center
+                sides = [pltpu.roll(c2, 1, 1) + c1, c0 + c2, c1 + pltpu.roll(c0, LANES - 1, 1)]
+                for t in range(3):
+                    xi[g, R, t] = (kk[q + 1, R, t] * center[t]
+                                   + kk[q, R, t] * ((north[t] + south[t]) + sides[t]))
+                north, center = center, south
+        pl.when(g >= 2)(lambda: out_copy(g - 2).wait())
+        slot = lax.rem(g, 2)
+        y = jnp.concatenate(
+            [jnp.concatenate([xi[g, HALO + r, t] for t in range(3)], axis=1) for r in range(rows)],
+            axis=0)
+        y = moved(y, back_ref[...], 2)
+        for r in range(rows):
+            for ct in range(2):
+                stage[slot, pl.ds(row_at(r, ct), SUB, stride=64), :] = (
+                    y[SUB * r:SUB * r + SUB, ct * LANES:(ct + 1) * LANES])
+        out_copy(g).start()
+        return c
+
+    def chunk(c, carry):
+        wait_rows(row_copies(c))
+        lax.fori_loop(c * CHUNK, (c + 1) * CHUNK, diffuse, 0)
+        return carry
+
+    lax.fori_loop(0, chunks, chunk, 0)
+    out_copy(fields8 - 2).wait()
+    out_copy(fields8 - 1).wait()
     every = got.at[pl.ds(1, n - 1), pl.ds(0, 5)]
-    pltpu.make_async_remote_copy(
-        src_ref=every, dst_ref=every, send_sem=send_sem, recv_sem=recv_sem.at[0],
-        device_id=place(1)[1], device_id_type=MESH).wait_send()
-
-
-def route(windows, kap, whole, n_lat, n_lon):
+    remote(every, every, send_sem, recv_sem.at[0], place(1)[1]).wait_send()
+
+
+def whole(windows, kap, view, mats, n_lat, n_lon):
     rows = kap.shape[0]
     ext = rows + 2 * HALO
+    g = view.shape[0] // 512
     spec = pl.BlockSpec(memory_space=pltpu.VMEM)
+    hbm = pl.BlockSpec(memory_space=pl.ANY)
     halo = [pltpu.VMEM((ext, 4, w * LANES), F32) for w in (2, 1, 1)]
+    dma = pltpu.SemaphoreType.DMA
     return pl.pallas_call(
-        lambda *refs: route_kernel(n_lat, n_lon, *refs),
-        out_shape=(jax.ShapeDtypeStruct((4, ext, 3, SUB, LANES), F32),
-                   jax.ShapeDtypeStruct((ext, 3, SUB, LANES), F32)),
-        in_specs=[spec] * 3,
-        out_specs=(spec, spec),
+        lambda *refs: whole_kernel(n_lat, n_lon, *refs),
+        out_shape=jax.ShapeDtypeStruct(view.shape, F32),
+        in_specs=[spec, spec, hbm] + [spec] * 3,
+        out_specs=hbm,
         scratch_shapes=[
+            pltpu.VMEM(view.shape, F32),
+            pltpu.VMEM((g, ext, 3, SUB, LANES), F32),
+        ] + [pltpu.VMEM((g, HALO, 2, SUB, LANES), F32)] * 4
+        + [pltpu.VMEM((g, 2, SUB, LANES), F32)] * 4
+        + [pltpu.VMEM((g, SUB, LANES), F32)] * 4 + [
+            pltpu.VMEM((2, 512, LANES), F32),
+            pltpu.VMEM((4, ext, 3, SUB, LANES), F32),
+            pltpu.VMEM((ext, 3, SUB, LANES), F32),
             pltpu.VMEM(windows.shape, F32),
             pltpu.VMEM((SUB * rows, 2 * LANES), F32),
             pltpu.VMEM((rows, 4, 2 * LANES), F32),
-        ] + halo + halo + [
-            pltpu.SemaphoreType.DMA, pltpu.SemaphoreType.DMA((8,)),
-        ] + [pltpu.SemaphoreType.DMA((8,))] * 4,
-        compiler_params=vmem(48, collective_id=0, has_side_effects=True),
-        name="route",
-    )(windows, kap, whole)
-
-
-def diffuse_kernel(p_ref, nh_ref, sh_ref, pw_ref, pe_ref, cn_ref, cs_ref, adj_ref, kk_ref,
-                   into_ref, back_ref, out_ref, x_ref):
-    rows = 32
-    ext = rows + 2 * HALO
-    group = iota((SUB, LANES), 1) // SUB
-
-    def lines(g, R):
-        r = R - HALO
-        if r < 0:
-            mid = [nh_ref[g, R, ct] for ct in range(2)]
-            w, w_at, e, e_at = cn_ref[g], 10 + R, cn_ref[g], 2 + R
-        elif r >= rows:
-            mid = [sh_ref[g, r - rows, ct] for ct in range(2)]
-            w, w_at, e, e_at = cs_ref[g], r - rows, cs_ref[g], 8 + r - rows
-        else:
-            mid = [p_ref[pl.ds(512 * g + row_at(r, ct), SUB, stride=64), :] for ct in range(2)]
-            w, w_at, e, e_at = pw_ref[g, r // 16], r % 16, pe_ref[g, r // 16], r % 16
-        w = jnp.where(group == w_at, w, 0.0)
-        e = jnp.where(group == e_at, e, 0.0)
-        return jnp.concatenate(mid + [w, e], axis=1)
-
-    for g in range(nh_ref.shape[0]):
-        for start in range(0, ext, ext // 2):
-            x = jnp.concatenate([lines(g, R) for R in range(start, start + ext // 2)], axis=0)
-            x = moved(x, into_ref[...], 2)
-            for i in range(ext // 2):
-                for t in range(3):
-                    x_ref[start + i, t] = (
-                        x[SUB * i:SUB * i + SUB, t * LANES:(t + 1) * LANES] * adj_ref[start + i, t])
-        for step in range(1, 2 * STEPS + 1):
-            q = 0 if step <= STEPS else 2
-            north = [x_ref[step - 1, t] for t in range(3)]
-            center = [x_ref[step, t] for t in range(3)]
-            for R in range(step, ext - step):
-                south = [x_ref[R + 1, t] for t in range(3)]
-                c0, c1, c2 = center
-                sides = [pltpu.roll(c2, 1, 1) + c1, c0 + c2, c1 + pltpu.roll(c0, LANES - 1, 1)]
-                for t in range(3):
-                    x_ref[R, t] = (kk_ref[q + 1, R, t] * center[t]
-                                   + kk_ref[q, R, t] * ((north[t] + south[t]) + sides[t]))
-                north, center = center, south
-        for start in range(0, rows, rows // 2):
-            y = jnp.concatenate(
-                [jnp.concatenate([x_ref[HALO + r, t] for t in range(3)], axis=1)
-                 for r in range(start, start + rows // 2)], axis=0)
-            y = moved(y, back_ref[...], 2)
-            for i in range(rows // 2):
-                for ct in range(2):
-                    out_ref[pl.ds(512 * g + row_at(start + i, ct), SUB, stride=64), :] = (
-                        y[SUB * i:SUB * i + SUB, ct * LANES:(ct + 1) * LANES])
-
-
-def diffuse(view, nh, sh, pw, pe, cn, cs, adj, kk, into, back):
-    groups = nh.shape[0]
-    per = 2
-    row_spec = pl.BlockSpec((per, HALO, 2, SUB, LANES), lambda g: (g, 0, 0, 0, 0))
-    col_spec = pl.BlockSpec((per, 2, SUB, LANES), lambda g: (g, 0, 0, 0))
-    corner_spec = pl.BlockSpec((per, SUB, LANES), lambda g: (g, 0, 0))
-    tile_spec = pl.BlockSpec((per * 512, LANES), lambda g: (g, 0))
-    fixed = [pl.BlockSpec(a.shape, lambda g, nd=a.ndim: (0,) * nd) for a in (adj, kk, into, back)]
-    return pl.pallas_call(
-        diffuse_kernel,
-        grid=(groups // per,),
-        out_shape=jax.ShapeDtypeStruct(view.shape, F32),
-        in_specs=[tile_spec, row_spec, row_spec, col_spec, col_spec, corner_spec, corner_spec] + fixed,
-        out_specs=tile_spec,
-        scratch_shapes=[pltpu.VMEM(adj.shape, F32)],
-        compiler_params=vmem(48),
-        name="diffuse",
-    )(view, nh, sh, pw, pe, cn, cs, adj, kk, into, back)
+        ] + halo + halo + [dma, dma((8,))] + [dma((8,))] * 4
+        + [dma((2, g // CHUNK))] * 2 + [dma((2,))] * 4 + [dma, dma((2,))],
+        compiler_params=vmem(60, collective_id=0, has_side_effects=True),
+        name="whole",
+    )(windows, kap, view, *mats)
 
 
 def shards(innovation, jacobian, channel_count, owner, footprint, weight, perturbation,
@@ -464,28 +515,11 @@
     view = perturbation.reshape(fields, rows // SUB, SUB, cols // LANES, LANES)
     view = view.transpose(0, 1, 3, 2, 4).reshape(fields * 64, LANES)
 
-    north, south, west, east = edges(view, fields // SUB)
-    down = [(i, i + 1) for i in range(n_lat - 1)]
-    up = [(i + 1, i) for i in range(n_lat - 1)]
-    right = [(i, (i + 1) % n_lon) for i in range(n_lon)]
-    left = [((i + 1) % n_lon, i) for i in range(n_lon)]
-    pe = lax.ppermute(west, "lon", left)
-    pw = lax.ppermute(east, "lon", right)
-    nh = lax.ppermute(south, "lat", down)
-    sh = lax.ppermute(north, "lat", up)
-    lane = lax.broadcasted_iota(I32, (1, SUB, LANES), 2)
-    top = jnp.where(lane < 48, pw[:, 0], jnp.roll(pe[:, 0], 64, axis=2))
-    bottom = jnp.where(lane >= 80, pw[:, 1], jnp.roll(pe[:, 1], 64, axis=2))
-    cs = lax.ppermute(top, "lat", up)
-    cn = lax.ppermute(bottom, "lat", down)
-
     windows = pack(innovation, jacobian, channel_count.reshape(1, obs), owner.reshape(1, obs),
                    footprint, weight)
     kap = jnp.stack([scale_first, 1.0 - 4.0 * scale_first, scale_second, 1.0 - 4.0 * scale_second],
                     axis=1)
-    into, whole, back = layouts()
-    kk, adj = route(windows.reshape(n_lat * n_lon, 6, 4, LANES), kap, whole, n_lat, n_lon)
-    out = diffuse(view, nh, sh, pw, pe, cn, cs, adj, kk, into, back)
+    out = whole(windows.reshape(n_lat * n_lon, 6, 4, LANES), kap, view, layouts(), n_lat, n_lon)
     out = out.reshape(fields, rows // SUB, cols // LANES, SUB, LANES).transpose(0, 1, 3, 2, 4)
     return out.reshape(members, levels, rows, cols)
 

time: 160 us -> 144 us (0.900); the launches traced: 157 us -> 143 us
  starting transfers between devices: 13.6 us -> 0 us
  Pallas kernels: 140 us -> 127 us
  local copies, waits for them, and re-layouts: 2.81 us -> 14.3 us
  other arithmetic: 0.26 us -> 2.31 us
    ppermute x6 -> x0, starting transfers between devices: 13.6 us -> none  [the longest x1 4.63 us: shards(): cn = lax.ppermute(bottom, 'lat', down)]
    pallas_call x3 -> x1, Pallas kernels: 128 us -> 114 us  [whole(): pl.pallas_call(lambda *refs: whole_kernel(n_lat, n_lon, *refs), out_shape...]
    unnamed x24 -> x15, local copies, waits for them, and re-layouts: 2.54 us -> 12.7 us
  transfers between devices with their start and end apart: 6 -> 0, of which waited for: 0 -> 0; matrix products, arithmetic and copies ran while one was open for 0% -> 0% of each run, Pallas kernels for 67% -> 0%
where the time goes in v3:
time: 144 us; the launch traced here: 143 us
  Pallas kernels  127 us (88%)
  local copies, waits for them, and re-layouts  14.3 us (10%)
  other arithmetic  2.31 us (2%)
    pallas_call x1, Pallas kernels, whole(): pl.pallas_call(lambda *refs: whole_kernel(n_lat, n_lon, *refs), out_shape...  114 us
    unnamed x15, local copies, waits for them, and re-layouts  12.7 us
    pallas_call x1, Pallas kernels, pack(): pl.pallas_call(pack_kernel, out_shape=jax.ShapeDtypeStruct((24 * LANES, L...  12.4 us

profile of v3, /device:TPU:1, one launch (start us, length us, event | category | flops | bytes accessed | tf_op | source)
XLA Modules:
  0.0 143.4 jit_solution(15582371094078446483)
XLA Ops:
  0.0 0.8 subtract_bitcast_fusion
  0.8 0.8 stack.15
  1.6 0.8 multiply_subtract_fusion
  2.4 0.8 stack.17
  3.2 0.8 pad_maximum_fusion.refs_1_
  4.0 0.0 copy-start.1
  4.0 1.6 %copy-done.1 = f32[32,4,4096]{2,1,0:T(4,128)S(1)} copy-done((f32[32,4,4096]{2,1,0:T(4,128)S(1)}, f32[32,4,4096]{2,1,0:T(4,128)}, u32[]{:S(2)}) %copy-start.1) | copy-done | bytes 2097176
  5.5 0.0 copy-start.2
  5.5 1.0 copy-done.2
  6.6 0.0 copy-start.3
  6.6 0.9 copy-done.3
  7.5 0.0 copy-start.4
  7.5 0.9 copy-done.4
  8.4 0.0 copy-start.5
  8.4 0.7 copy-done.5
  9.1 0.0 copy-start.6
  9.1 0.7 copy-done.6
  9.8 12.4 %pack.1 = f32[3072,128]{1,0:T(8,128)S(1)} custom-call(f32[32,4096]{1,0:T(8,128)S(1)} %copy-done.2, f32[32,4,4096]{2,1,0:T(4,128)S(1)} %copy-done.1, s32[1,4096]{1,0:T(1,128)S(1)} %bitcast.16, s32[1,4096]{1,0:T(1,128)S(1)} %bitcast.17, s32[8,4096]{1,0:T(8,128)S(1)} %copy-done.3, f32[8,4096]{1,0:T(8,128)S(1)} %copy-done.4), custom_call_target="tpu_custom_call" | custom-call | tf_op jit(solution)/shard_map/pack/pallas_call | solution.py:116
  22.2 0.0 copy-start
  22.3 1.1 copy-done
  23.4 114.3 %whole.1 = f32[10240,128]{1,0:T(8,128)} custom-call(f32[128,6,4,128]{3,2,1,0:T(4,128)} %bitcast.15, f32[32,4,256]{2,1,0:T(4,128)} %pad_maximum_fusion.refs_1_, f32[10240,128]{1,0:T(8,128)} %bitcast.19, bf16[1536,384]{1,0:T(8,128)(2,1)} %constant.10.clone.refs_3_, bf16[1024,384]{1,0:T(8,128)(2,1)} %constant.11.clone.refs_4_, ...), custom_call_target="tpu_custom_call" | custom-call | tf_op jit(solution)/shard_map/whole/pallas_call | solution.py:485
  137.7 5.7 %copy.15 = f32[40,4,32,256]{3,2,1,0:T(8,128)} copy(f32[40,4,32,256]{3,2,1,0:T(8,128)} %bitcast.18) | data formatting | bytes 10485760
  (2 shorter events, 0.1 us)
Async XLA Ops:
  4.0 1.6 %copy-start.1 = (f32[32,4,4096]{2,1,0:T(4,128)S(1)}, f32[32,4,4096]{2,1,0:T(4,128)}, u32[]{:S(2)}) copy-start(f32[32,4,4096]{2,1,0:T(4,128)} %jac_ref.1) | copy-start | bytes 6291460
  5.5 1.0 copy-start.2
  6.6 0.9 copy-start.3
  7.5 0.9 copy-start.4
  8.4 0.7 copy-start.5
  9.1 0.7 copy-start.6
  22.2 1.1 copy-start

commit v4 on v3

--- a/solution.py
+++ b/solution.py
@@ -37,42 +37,50 @@
     return (r // SUB) * 16 + ct * SUB + r % SUB
 
 
-def pack_kernel(inn_ref, jac_ref, cc_ref, own_ref, foot_ref, wgt_ref, out_ref,
-                tot_ref, acc_ref, sorted_ref, cnt_v, cnt_s, sem):
+def pack_kernel(inn_h, jac_h, cc_h, own_h, foot_h, wgt_h, out_ref,
+                inn_ref, jac_ref, cc_ref, own_ref, foot_ref, wgt_ref,
+                tot_ref, acc_ref, sorted_ref, cnt_v, cnt_s, sem, in_sem):
     chans, obs = inn_ref.shape
     blk = 256
-    ones = jnp.ones((2 * blk, LANES), BF16)
-    ones8 = jnp.ones((SUB, 2 * blk), BF16)
-    tot_ref[...] = jnp.zeros_like(tot_ref)
-
-    def count(i, row):
-        own = own_ref[:, pl.ds(pl.multiple_of(i * 2 * blk, 2 * blk), 2 * blk)]
-        hot = (iota((LANES, 2 * blk), 0) == own).astype(F32).astype(BF16)
-        tot_ref[...] += dot(hot, ones)
-        return row + dot_nt(ones8, hot)
-
-    tot_row = lax.fori_loop(0, obs // (2 * blk), count, jnp.zeros((SUB, LANES), F32))
+    wide = 4 * blk
+    loads = [pltpu.make_async_copy(h, v, in_sem.at[i]) for i, (h, v) in enumerate((
+        (own_h, own_ref), (inn_h, inn_ref), (jac_h, jac_ref), (cc_h, cc_ref),
+        (foot_h, foot_ref), (wgt_h, wgt_ref)))]
+    for copy in loads:
+        copy.start()
+    loads[0].wait()
+    hot_all = (iota((LANES, obs), 0) == own_ref[...]).astype(F32).astype(BF16)
+    totals = dot(hot_all, jnp.ones((obs, LANES), BF16))
+    tot_row = dot_nt(jnp.ones((SUB, obs), BF16), hot_all)
     upper = (iota((LANES, LANES), 0) < iota((LANES, LANES), 1)).astype(F32).astype(BF16)
     lower = (iota((LANES, LANES), 0) > iota((LANES, LANES), 1)).astype(F32).astype(BF16)
     cnt_v[0:SUB] = dot(tot_row.astype(BF16), upper).astype(I32)
     cnt_v[SUB:2 * SUB] = tot_row.astype(I32)
     to_smem = pltpu.make_async_copy(cnt_v, cnt_s, sem)
     to_smem.start()
-    tot_ref[...] = dot(lower, tot_ref[...].astype(BF16))
+    tot_ref[...] = dot(lower, totals.astype(BF16))
     upper_b = (iota((blk, blk), 0) < iota((blk, blk), 1)).astype(F32).astype(BF16)
     acc_ref[...] = jnp.zeros_like(acc_ref)
+    for copy in loads[1:]:
+        copy.wait()
 
     def block(i, carry):
-        at = pl.ds(pl.multiple_of(i * blk, blk), blk)
+        at = pl.ds(pl.multiple_of(i * wide, wide), wide)
         own = own_ref[:, at]
-        hot = iota((LANES, blk), 0) == own
-        hot_b = hot.astype(F32).astype(BF16)
+        hots = [iota((LANES, blk), 0) == own[:, j * blk:(j + 1) * blk] for j in range(4)]
+        stack = jnp.concatenate([h.astype(F32).astype(BF16) for h in hots], axis=0)
+        ranks = dot(stack, upper_b)
+        sums = dot(stack, jnp.ones((blk, LANES), BF16))
         base = tot_ref[...]
-        place = dot(hot_b, upper_b) + jnp.concatenate([base, base], axis=1)
-        tot_ref[...] = base + dot(hot_b, ones[:blk])
-        pos = jnp.sum(jnp.where(hot, place, 0.0), axis=0, keepdims=True).astype(I32)
+        places = []
+        for j in range(4):
+            rank = ranks[LANES * j:LANES * (j + 1)] + jnp.concatenate([base, base], axis=1)
+            places.append(jnp.sum(jnp.where(hots[j], rank, 0.0), axis=0, keepdims=True))
+            base = base + sums[LANES * j:LANES * (j + 1)]
+        tot_ref[...] = base
+        pos = jnp.concatenate(places, axis=1).astype(I32)
         cc = cc_ref[:, at]
-        prof = jnp.zeros((4, blk), F32)
+        prof = jnp.zeros((4, wide), F32)
         for c in range(chans):
             live = jnp.where(cc > c, inn_ref[c:c + 1, at], 0.0)
             prof = prof + jac_ref[c, :, at] * live
@@ -81,12 +89,13 @@
         both = jnp.concatenate([head, full - head], axis=0)
         hi = lax.shift_right_logical(pos, 8)
         lo = lax.bitwise_and(pos, 255)
-        spread = jnp.concatenate([jnp.where(hi == h, both, 0.0) for h in range(obs // blk)], axis=0)
-        hot_lo = (iota((blk, blk), 0) == lo).astype(F32).astype(BF16)
-        acc_ref[...] += dot_nt(spread.astype(BF16), hot_lo)
+        spread = jnp.concatenate(
+            [jnp.where(hi == h, both, 0.0).astype(BF16) for h in range(obs // blk)], axis=0)
+        hot_lo = (iota((blk, wide), 0) == lo).astype(F32).astype(BF16)
+        acc_ref[...] += dot_nt(spread, hot_lo)
         return carry
 
-    lax.fori_loop(0, obs // blk, block, 0)
+    lax.fori_loop(0, obs // wide, block, 0)
     for h in range(obs // blk):
         s = acc_ref[48 * h:48 * h + 24, :] + acc_ref[48 * h + 24:48 * h + 48, :]
         sorted_ref[2 * h] = s[:, :LANES]
@@ -116,17 +125,18 @@
     return pl.pallas_call(
         pack_kernel,
         out_shape=jax.ShapeDtypeStruct((24 * LANES, LANES), F32),
-        in_specs=[pl.BlockSpec(memory_space=pltpu.VMEM)] * 6,
+        in_specs=[pl.BlockSpec(memory_space=pl.ANY)] * 6,
         out_specs=pl.BlockSpec(memory_space=pltpu.VMEM),
-        scratch_shapes=[
+        scratch_shapes=[pltpu.VMEM(a.shape, a.dtype) for a in (inn, jac, cc, own, foot, wgt)] + [
             pltpu.VMEM((LANES, LANES), F32),
             pltpu.VMEM((48 * (obs // 256), 256), F32),
             pltpu.VMEM((obs // LANES + 2, 24, LANES), F32),
             pltpu.VMEM((2 * SUB, LANES), I32),
             pltpu.SMEM((2 * SUB, LANES), I32),
             pltpu.SemaphoreType.DMA,
+            pltpu.SemaphoreType.DMA((6,)),
         ],
-        compiler_params=vmem(40),
+        compiler_params=vmem(60),
         name="pack",
     )(inn, jac, cc, own, foot, wgt)
 
@@ -223,8 +233,8 @@
 BATCH = 8
 
 
-def whole_kernel(n_lat, n_lon, s_ref, kap_ref, p_hbm, whole_ref, into_ref, back_ref, o_hbm,
-                 pv, xi, nsend, ssend, nh, sh, wsend, esend, pw, pe, tsend, bsend, cs, cn, stage,
+def whole_kernel(n_lat, n_lon, s_ref, k1_ref, k2_ref, p_hbm, whole_ref, into_ref, o_hbm,
+                 kap_ref, pv, xi, nsend, ssend, nh, sh, wsend, esend, pw, pe, tsend, bsend, cs, cn,
                  kk, adj, got, acc, sums, mid, wb, eb, mid2, wb2, eb2,
                  send_sem, recv_sem, hs, hr, hs2, hr2, row_s, row_r, col_s, col_r, cor_s, cor_r,
                  in_sem, out_sem):
@@ -252,6 +262,9 @@
         return c
 
     lax.fori_loop(1, n, signal, 0)
+    for r in range(rows):
+        k1, k2 = k1_ref[r:r + 1, :], k2_ref[r:r + 1, :]
+        kap_ref[r] = jnp.concatenate([k1, 1.0 - 4.0 * k1, k2, 1.0 - 4.0 * k2], axis=0)
 
     @pl.when(lat == 0)
     def _():
@@ -355,17 +368,22 @@
         return jnp.concatenate(
             mid_rows + [jnp.where(group == w_at, w, 0.0), jnp.where(group == e_at, e, 0.0)], axis=1)
 
-    def inner(g, c):
+    def inner(c, carry):
         x = jnp.concatenate(
-            [one([point(g, r, 0), point(g, r, 1)], pw[g, r // 16], r % 16, pe[g, r // 16], r % 16)
-             for r in range(rows)], axis=0)
+            [one([point(c * CHUNK + u, r, 0), point(c * CHUNK + u, r, 1)],
+                 pw[c * CHUNK + u, r // 16], r % 16, pe[c * CHUNK + u, r // 16], r % 16)
+             for u in range(CHUNK) for r in range(rows)], axis=0)
         x = moved(x, into_ref[...], 2)
-        for r in range(rows):
-            for t in range(3):
-                xi[g, HALO + r, t] = x[SUB * r:SUB * r + SUB, t * LANES:(t + 1) * LANES]
-        return c
-
-    lax.fori_loop(0, fields8, inner, 0)
+        for u in range(CHUNK):
+            for r in range(rows):
+                i = SUB * (u * rows + r)
+                for t in range(3):
+                    xi[c * CHUNK + u, HALO + r, t] = x[i:i + SUB, t * LANES:(t + 1) * LANES]
+        return carry
+
+    for c in range(1, 3):
+        start_rows(row_copies(c))
+    lax.fori_loop(0, chunks, inner, 0)
 
     sub = iota((SUB, LANES), 0)
     row_ids = (iota((2 * LANES, LANES), 0) // SUB).astype(F32).astype(BF16)
@@ -398,7 +416,7 @@
         acc[...] += dot_nt(jnp.concatenate(left, axis=1), jnp.concatenate(right, axis=1))
         return c
 
-    when_sent = {2: [1], 4: [2], 6: [3, 4]}
+    when_sent = {0: [3], 1: [4]}
     for g in range(groups):
         first, last = max(1, g * per), (g + 1) * per
         part = got.at[pl.ds(first, last - first), pl.ds(0, 5)]
@@ -421,20 +439,8 @@
 
     wait_rows(corners)
 
-    def out_copy(g):
-        slot = lax.rem(g, 2)
-        return pltpu.make_async_copy(
-            stage.at[slot], o_hbm.at[pl.ds(512 * g, 512)], out_sem.at[slot])
-
     def diffuse(g, c):
-        lines = [one([nh[g, j, 0], nh[g, j, 1]], cn[g], 10 + j, cn[g], 2 + j) for j in range(HALO)]
-        lines += [one([sh[g, j, 0], sh[g, j, 1]], cs[g], j, cs[g], 8 + j) for j in range(HALO)]
-        x = moved(jnp.concatenate(lines, axis=0), into_ref[...], 2)
-        for j in range(2 * HALO):
-            R = j if j < HALO else rows + j
-            for t in range(3):
-                xi[g, R, t] = x[SUB * j:SUB * j + SUB, t * LANES:(t + 1) * LANES] * adj[R, t]
-        for R in range(HALO, HALO + rows):
+        for R in range(ext):
             for t in range(3):
                 xi[g, R, t] = xi[g, R, t] * adj[R, t]
         for step in range(1, 2 * STEPS + 1):
@@ -449,33 +455,39 @@
                     xi[g, R, t] = (kk[q + 1, R, t] * center[t]
                                    + kk[q, R, t] * ((north[t] + south[t]) + sides[t]))
                 north, center = center, south
-        pl.when(g >= 2)(lambda: out_copy(g - 2).wait())
-        slot = lax.rem(g, 2)
-        y = jnp.concatenate(
-            [jnp.concatenate([xi[g, HALO + r, t] for t in range(3)], axis=1) for r in range(rows)],
-            axis=0)
-        y = moved(y, back_ref[...], 2)
-        for r in range(rows):
-            for ct in range(2):
-                stage[slot, pl.ds(row_at(r, ct), SUB, stride=64), :] = (
-                    y[SUB * r:SUB * r + SUB, ct * LANES:(ct + 1) * LANES])
-        out_copy(g).start()
         return c
 
     def chunk(c, carry):
         wait_rows(row_copies(c))
+        lines = []
+        for u in range(CHUNK):
+            g = c * CHUNK + u
+            lines += [one([nh[g, j, 0], nh[g, j, 1]], cn[g], 10 + j, cn[g], 2 + j) for j in range(HALO)]
+            lines += [one([sh[g, j, 0], sh[g, j, 1]], cs[g], j, cs[g], 8 + j) for j in range(HALO)]
+        x = moved(jnp.concatenate(lines, axis=0), into_ref[...], 2)
+        for u in range(CHUNK):
+            for j in range(2 * HALO):
+                R = j if j < HALO else rows + j
+                i = SUB * (u * 2 * HALO + j)
+                for t in range(3):
+                    xi[c * CHUNK + u, R, t] = x[i:i + SUB, t * LANES:(t + 1) * LANES]
         lax.fori_loop(c * CHUNK, (c + 1) * CHUNK, diffuse, 0)
+        done(c).start()
         return carry
 
+    def done(c):
+        at = pl.ds(c * CHUNK, CHUNK)
+        return pltpu.make_async_copy(xi.at[at, pl.ds(HALO, rows)], o_hbm.at[at], out_sem.at[c])
+
     lax.fori_loop(0, chunks, chunk, 0)
-    out_copy(fields8 - 2).wait()
-    out_copy(fields8 - 1).wait()
+    for c in range(chunks):
+        done(c).wait()
     every = got.at[pl.ds(1, n - 1), pl.ds(0, 5)]
     remote(every, every, send_sem, recv_sem.at[0], place(1)[1]).wait_send()
 
 
-def whole(windows, kap, view, mats, n_lat, n_lon):
-    rows = kap.shape[0]
+def whole(windows, k1, k2, view, mats, n_lat, n_lon):
+    rows = k1.shape[0]
     ext = rows + 2 * HALO
     g = view.shape[0] // 512
     spec = pl.BlockSpec(memory_space=pltpu.VMEM)
@@ -484,26 +496,55 @@
     dma = pltpu.SemaphoreType.DMA
     return pl.pallas_call(
         lambda *refs: whole_kernel(n_lat, n_lon, *refs),
-        out_shape=jax.ShapeDtypeStruct(view.shape, F32),
-        in_specs=[spec, spec, hbm] + [spec] * 3,
+        out_shape=jax.ShapeDtypeStruct((g, rows, 3, SUB, LANES), F32),
+        in_specs=[spec, spec, spec, hbm, spec, spec],
         out_specs=hbm,
         scratch_shapes=[
+            pltpu.VMEM((rows, 4, 2 * LANES), F32),
             pltpu.VMEM(view.shape, F32),
             pltpu.VMEM((g, ext, 3, SUB, LANES), F32),
         ] + [pltpu.VMEM((g, HALO, 2, SUB, LANES), F32)] * 4
         + [pltpu.VMEM((g, 2, SUB, LANES), F32)] * 4
         + [pltpu.VMEM((g, SUB, LANES), F32)] * 4 + [
-            pltpu.VMEM((2, 512, LANES), F32),
             pltpu.VMEM((4, ext, 3, SUB, LANES), F32),
             pltpu.VMEM((ext, 3, SUB, LANES), F32),
             pltpu.VMEM(windows.shape, F32),
             pltpu.VMEM((SUB * rows, 2 * LANES), F32),
             pltpu.VMEM((rows, 4, 2 * LANES), F32),
         ] + halo + halo + [dma, dma((8,))] + [dma((8,))] * 4
-        + [dma((2, g // CHUNK))] * 2 + [dma((2,))] * 4 + [dma, dma((2,))],
+        + [dma((2, g // CHUNK))] * 2 + [dma((2,))] * 4 + [dma, dma((g // CHUNK,))],
         compiler_params=vmem(60, collective_id=0, has_side_effects=True),
         name="whole",
-    )(windows, kap, view, *mats)
+    )(windows, k1, k2, view, *mats)
+
+
+def finish_kernel(x_ref, back_ref, o_ref):
+    per, rows = x_ref.shape[:2]
+    y = jnp.concatenate(
+        [jnp.concatenate([x_ref[u, r, t] for t in range(3)], axis=1)
+         for u in range(per) for r in range(rows)], axis=0)
+    y = moved(y, back_ref[...], 2)
+    for u in range(per):
+        for r in range(rows):
+            i = SUB * (u * rows + r)
+            for ct in range(2):
+                o_ref[pl.ds(512 * u + row_at(r, ct), SUB, stride=64), :] = (
+                    y[i:i + SUB, ct * LANES:(ct + 1) * LANES])
+
+
+def finish(x, back):
+    g, rows = x.shape[:2]
+    per = 2
+    return pl.pallas_call(
+        finish_kernel,
+        grid=(g // per,),
+        out_shape=jax.ShapeDtypeStruct((g * 512, LANES), F32),
+        in_specs=[pl.BlockSpec((per,) + x.shape[1:], lambda i: (i, 0, 0, 0, 0)),
+                  pl.BlockSpec(back.shape, lambda i: (0, 0))],
+        out_specs=pl.BlockSpec((per * 512, LANES), lambda i: (i, 0)),
+        compiler_params=vmem(40),
+        name="finish",
+    )(x, back)
 
 
 def shards(innovation, jacobian, channel_count, owner, footprint, weight, perturbation,
@@ -517,9 +558,10 @@
 
     windows = pack(innovation, jacobian, channel_count.reshape(1, obs), owner.reshape(1, obs),
                    footprint, weight)
-    kap = jnp.stack([scale_first, 1.0 - 4.0 * scale_first, scale_second, 1.0 - 4.0 * scale_second],
-                    axis=1)
-    out = whole(windows.reshape(n_lat * n_lon, 6, 4, LANES), kap, view, layouts(), n_lat, n_lon)
+    *mats, back = layouts()
+    out = whole(windows.reshape(n_lat * n_lon, 6, 4, LANES), scale_first, scale_second, view, mats,
+                n_lat, n_lon)
+    out = finish(out, back)
     out = out.reshape(fields, rows // SUB, cols // LANES, SUB, LANES).transpose(0, 1, 3, 2, 4)
     return out.reshape(members, levels, rows, cols)
 

time: 144 us -> 121 us (0.84)
  local copies, waits for them, and re-layouts: 14.3 us -> 3.23 us
  Pallas kernels: 127 us -> 118 us
  other arithmetic: 2.31 us -> 0 us
    pallas_call x1, Pallas kernels: 114 us -> 101 us  [whole(): pl.pallas_call(lambda *refs: whole_kernel(n_lat, n_lon, *refs), out_shape...]
    unnamed x15 -> x4, local copies, waits for them, and re-layouts: 12.7 us -> 3.23 us
    pallas_call x0 -> x1, Pallas kernels: none -> 7.61 us  [finish(): pl.pallas_call(finish_kernel, grid=(g // per,), out_shape=jax.ShapeDtypeS...]
    pallas_call x1, Pallas kernels: 12.4 us -> 9.34 us  [pack(): pl.pallas_call(pack_kernel, out_shape=jax.ShapeDtypeStruct((24 * LANES, L...]
    another operation x4 -> x0, local copies, waits for them, and re-layouts: 1.63 us -> none  [shards(): jnp.stack([scale_first, 1.0 - 4.0 * scale_first, scale_second, 1.0 - 4.0...]
    another operation x2 -> x0, other arithmetic: 1.55 us -> none  [shards(): jnp.stack([scale_first, 1.0 - 4.0 * scale_first, scale_second, 1.0 - 4.0...]
where the time goes in v4:
time: 121 us
  Pallas kernels  118 us (98%)
  local copies, waits for them, and re-layouts  3.23 us (3%)
    pallas_call x1, Pallas kernels, whole(): pl.pallas_call(lambda *refs: whole_kernel(n_lat, n_lon, *refs), out_shape...  101 us
    pallas_call x1, Pallas kernels, pack(): pl.pallas_call(pack_kernel, out_shape=jax.ShapeDtypeStruct((24 * LANES, L...  9.34 us
    pallas_call x1, Pallas kernels, finish(): pl.pallas_call(finish_kernel, grid=(g // per,), out_shape=jax.ShapeDtypeS...  7.61 us
    unnamed x4, local copies, waits for them, and re-layouts  3.23 us

profile of v4, /device:TPU:1, one launch (start us, length us, event | category | flops | bytes accessed | tf_op | source)
XLA Modules:
  0.0 121.0 jit_solution(16566696486150572187)
XLA Ops:
  0.0 9.3 %pack.1 = f32[3072,128]{1,0:T(8,128)} custom-call(f32[32,4096]{1,0:T(8,128)} %inn_h.1, f32[32,4,4096]{2,1,0:T(4,128)} %jac_h.1, s32[1,4096]{1,0:T(1,128)} %bitcast.15, s32[1,4096]{1,0:T(1,128)} %bitcast.16, s32[8,4096]{1,0:T(8,128)} %foot_h.1, f32[8,4096]{1,0:T(8,128)} %wgt_h.1), custom_call_target="tpu_custom_call" | custom-call | tf_op jit(solution)/shard_map/pack/pallas_call | solution.py:125
  9.3 0.0 copy-start.1
  9.4 100.8 %whole.1.x_ref = f32[20,32,3,8,128]{4,3,2,1,0:T(8,128)} custom-call(f32[128,6,4,128]{3,2,1,0:T(4,128)} %bitcast.13, f32[32,256]{1,0:T(8,128)} %refs_1_.1, f32[32,256]{1,0:T(8,128)} %refs_2_.1, f32[10240,128]{1,0:T(8,128)} %bitcast.14, bf16[1536,384]{1,0:T(8,128)(2,1)} %constant.6.clone.refs_4_, bf16[1024,384]{1,0:T(8,128)(2,1)} %constant.7.clone.refs_5_), custom_call_target="tpu_custom_call" | custom-call | tf_op jit(solution)/shard_map/whole/pallas_call | solution.py:497
  110.1 0.0 copy-done.1
  110.2 0.0 copy-start
  110.2 3.2 %copy-done = f32[20,32,3,8,128]{4,3,2,1,0:T(8,128)S(1)} copy-done((f32[20,32,3,8,128]{4,3,2,1,0:T(8,128)S(1)}, f32[20,32,3,8,128]{4,3,2,1,0:T(8,128)}, u32[]{:S(2)}) %copy-start) | copy-done | bytes 7864344
  113.4 7.6 %finish.1 = f32[10240,128]{1,0:T(8,128)} custom-call(f32[20,32,3,8,128]{4,3,2,1,0:T(8,128)S(1)} %copy-done, bf16[768,256]{1,0:T(8,128)(2,1)S(1)} %copy-done.1), custom_call_target="tpu_custom_call" | custom-call | tf_op jit(solution)/shard_map/finish/pallas_call | solution.py:538
Async XLA Ops:
  9.3 100.8 %copy-start.1 = (bf16[768,256]{1,0:T(8,128)(2,1)S(1)}, bf16[768,256]{1,0:T(8,128)(2,1)}, u32[]{:S(2)}) copy-start(bf16[768,256]{1,0:T(8,128)(2,1)} %constant.8.clone.back_ref) | copy-start | bytes 1179652
  110.2 3.2 %copy-start = (f32[20,32,3,8,128]{4,3,2,1,0:T(8,128)S(1)}, f32[20,32,3,8,128]{4,3,2,1,0:T(8,128)}, u32[]{:S(2)}) copy-start(f32[20,32,3,8,128]{4,3,2,1,0:T(8,128)} %whole.1.x_ref) | copy-start | bytes 23592964

commit v5 on v4

--- a/solution.py
+++ b/solution.py
@@ -231,9 +231,10 @@
 
 CHUNK = 4
 BATCH = 8
-
-
-def whole_kernel(n_lat, n_lon, s_ref, k1_ref, k2_ref, p_hbm, whole_ref, into_ref, o_hbm,
+MIX = 37
+
+
+def whole_kernel(n_lat, n_lon, s_ref, k1_ref, k2_ref, p_hbm, whole_ref, into_ref, back_ref, o_hbm,
                  kap_ref, pv, xi, nsend, ssend, nh, sh, wsend, esend, pw, pe, tsend, bsend, cs, cn,
                  kk, adj, got, acc, sums, mid, wb, eb, mid2, wb2, eb2,
                  send_sem, recv_sem, hs, hr, hs2, hr2, row_s, row_r, col_s, col_r, cor_s, cor_r,
@@ -279,15 +280,18 @@
     acc[...] = jnp.zeros_like(acc)
     pl.semaphore_wait(bar, n - 1)
 
-    for g in range(groups):
-        def send(k, c, g=g):
-            t, to = place(k)
+    def send_group(g, first=0):
+        def send(i, c):
+            t, to = place(lax.rem(MIX * i, n))
             pltpu.make_async_remote_copy(
-                src_ref=s_ref.at[t, pl.ds(0, 5)], dst_ref=got.at[k, pl.ds(0, 5)],
+                src_ref=s_ref.at[t, pl.ds(0, 5)], dst_ref=got.at[i, pl.ds(0, 5)],
                 send_sem=send_sem, recv_sem=recv_sem.at[g], device_id=to, device_id_type=MESH).start()
             return c
 
-        lax.fori_loop(max(1, g * per), (g + 1) * per, send, 0)
+        lax.fori_loop(g * per + first, (g + 1) * per, send, 0)
+
+    send_group(0, 1)
+    send_group(1)
     kap_copies = halo_copies(kap_ref, mid, wb, eb, hs, hr, n_lon)
     halo_start(kap_copies, lat, n_lat)
 
@@ -341,6 +345,7 @@
 
     for copy in cols:
         copy.start()
+    send_group(2)
     start_rows(row_copies(0))
 
     halo_wait(kap_copies, lat, n_lat)
@@ -379,10 +384,9 @@
                 i = SUB * (u * rows + r)
                 for t in range(3):
                     xi[c * CHUNK + u, HALO + r, t] = x[i:i + SUB, t * LANES:(t + 1) * LANES]
+        pl.when(c < 4)(lambda: send_group(3 + c))
         return carry
 
-    for c in range(1, 3):
-        start_rows(row_copies(c))
     lax.fori_loop(0, chunks, inner, 0)
 
     sub = iota((SUB, LANES), 0)
@@ -416,7 +420,8 @@
         acc[...] += dot_nt(jnp.concatenate(left, axis=1), jnp.concatenate(right, axis=1))
         return c
 
-    when_sent = {0: [3], 1: [4]}
+    send_group(7)
+    when_sent = {0: [1], 1: [2], 2: [3], 3: [4]}
     for g in range(groups):
         first, last = max(1, g * per), (g + 1) * per
         part = got.at[pl.ds(first, last - first), pl.ds(0, 5)]
@@ -472,12 +477,22 @@
                 for t in range(3):
                     xi[c * CHUNK + u, R, t] = x[i:i + SUB, t * LANES:(t + 1) * LANES]
         lax.fori_loop(c * CHUNK, (c + 1) * CHUNK, diffuse, 0)
+        y = jnp.concatenate(
+            [jnp.concatenate([xi[c * CHUNK + u, HALO + r, t] for t in range(3)], axis=1)
+             for u in range(CHUNK) for r in range(rows)], axis=0)
+        y = moved(y, back_ref[...], 2)
+        for u in range(CHUNK):
+            for r in range(rows):
+                i = SUB * (u * rows + r)
+                for ct in range(2):
+                    pv[pl.ds(512 * (c * CHUNK + u) + row_at(r, ct), SUB, stride=64), :] = (
+                        y[i:i + SUB, ct * LANES:(ct + 1) * LANES])
         done(c).start()
         return carry
 
     def done(c):
-        at = pl.ds(c * CHUNK, CHUNK)
-        return pltpu.make_async_copy(xi.at[at, pl.ds(HALO, rows)], o_hbm.at[at], out_sem.at[c])
+        at = pl.ds(c * CHUNK * 512, CHUNK * 512)
+        return pltpu.make_async_copy(pv.at[at], o_hbm.at[at], out_sem.at[c])
 
     lax.fori_loop(0, chunks, chunk, 0)
     for c in range(chunks):
@@ -496,8 +511,8 @@
     dma = pltpu.SemaphoreType.DMA
     return pl.pallas_call(
         lambda *refs: whole_kernel(n_lat, n_lon, *refs),
-        out_shape=jax.ShapeDtypeStruct((g, rows, 3, SUB, LANES), F32),
-        in_specs=[spec, spec, spec, hbm, spec, spec],
+        out_shape=jax.ShapeDtypeStruct(view.shape, F32),
+        in_specs=[spec, spec, spec, hbm, spec, spec, spec],
         out_specs=hbm,
         scratch_shapes=[
             pltpu.VMEM((rows, 4, 2 * LANES), F32),
@@ -518,33 +533,33 @@
     )(windows, k1, k2, view, *mats)
 
 
-def finish_kernel(x_ref, back_ref, o_ref):
-    per, rows = x_ref.shape[:2]
-    y = jnp.concatenate(
-        [jnp.concatenate([x_ref[u, r, t] for t in range(3)], axis=1)
-         for u in range(per) for r in range(rows)], axis=0)
-    y = moved(y, back_ref[...], 2)
-    for u in range(per):
-        for r in range(rows):
-            i = SUB * (u * rows + r)
-            for ct in range(2):
-                o_ref[pl.ds(512 * u + row_at(r, ct), SUB, stride=64), :] = (
-                    y[i:i + SUB, ct * LANES:(ct + 1) * LANES])
-
-
-def finish(x, back):
-    g, rows = x.shape[:2]
-    per = 2
+def place_kernel(x_ref, o_ref, buf, in_sem, out_sem):
+    count = in_sem.shape[0]
+    rows = x_ref.shape[0] // count
+    parts = [pl.ds(i * rows, rows) for i in range(count)]
+    loads = [pltpu.make_async_copy(x_ref.at[p], buf.at[p], in_sem.at[i]) for i, p in enumerate(parts)]
+    stores = [pltpu.make_async_copy(buf.at[p], o_ref.at[p], out_sem.at[i]) for i, p in enumerate(parts)]
+    for copy in loads:
+        copy.start()
+    for i in range(count):
+        loads[i].wait()
+        stores[i].start()
+    for copy in stores:
+        copy.wait()
+
+
+def placed(x):
+    hbm = pl.BlockSpec(memory_space=pl.ANY)
     return pl.pallas_call(
-        finish_kernel,
-        grid=(g // per,),
-        out_shape=jax.ShapeDtypeStruct((g * 512, LANES), F32),
-        in_specs=[pl.BlockSpec((per,) + x.shape[1:], lambda i: (i, 0, 0, 0, 0)),
-                  pl.BlockSpec(back.shape, lambda i: (0, 0))],
-        out_specs=pl.BlockSpec((per * 512, LANES), lambda i: (i, 0)),
-        compiler_params=vmem(40),
-        name="finish",
-    )(x, back)
+        place_kernel,
+        out_shape=jax.ShapeDtypeStruct(x.shape, F32),
+        in_specs=[hbm],
+        out_specs=hbm,
+        scratch_shapes=[pltpu.VMEM(x.shape, F32), pltpu.SemaphoreType.DMA((5,)),
+                        pltpu.SemaphoreType.DMA((5,))],
+        compiler_params=vmem(60),
+        name="placed",
+    )(x)
 
 
 def shards(innovation, jacobian, channel_count, owner, footprint, weight, perturbation,
@@ -558,10 +573,9 @@
 
     windows = pack(innovation, jacobian, channel_count.reshape(1, obs), owner.reshape(1, obs),
                    footprint, weight)
-    *mats, back = layouts()
-    out = whole(windows.reshape(n_lat * n_lon, 6, 4, LANES), scale_first, scale_second, view, mats,
+    out = whole(windows.reshape(n_lat * n_lon, 6, 4, LANES), scale_first, scale_second, view, layouts(),
                 n_lat, n_lon)
-    out = finish(out, back)
+    out = placed(out)
     out = out.reshape(fields, rows // SUB, cols // LANES, SUB, LANES).transpose(0, 1, 3, 2, 4)
     return out.reshape(members, levels, rows, cols)
 

time: 121 us -> 118 us (0.975)
  local copies, waits for them, and re-layouts: 3.23 us -> 0 us
    pallas_call x1, Pallas kernels: 101 us -> 104 us  [whole(): pl.pallas_call(lambda *refs: whole_kernel(n_lat, n_lon, *refs), out_shape...]
    unnamed x4 -> x0, local copies, waits for them, and re-layouts: 3.23 us -> none
    pallas_call x1, Pallas kernels: 7.61 us -> 4.38 us  [placed(): pl.pallas_call(place_kernel, out_shape=jax.ShapeDtypeStruct(x.shape, F32)...]
where the time goes in v5:
time: 118 us
  Pallas kernels  118 us (100%)
    pallas_call x1, Pallas kernels, whole(): pl.pallas_call(lambda *refs: whole_kernel(n_lat, n_lon, *refs), out_shape...  104 us
    pallas_call x1, Pallas kernels, pack(): pl.pallas_call(pack_kernel, out_shape=jax.ShapeDtypeStruct((24 * LANES, L...  9.33 us
    pallas_call x1, Pallas kernels, placed(): pl.pallas_call(place_kernel, out_shape=jax.ShapeDtypeStruct(x.shape, F32)...  4.38 us

profile of v5, /device:TPU:1, one launch (start us, length us, event | category | flops | bytes accessed | tf_op | source)
XLA Modules:
  0.0 117.9 jit_solution(5298915033053968465)
XLA Ops:
  0.0 9.3 %pack.1 = f32[3072,128]{1,0:T(8,128)} custom-call(f32[32,4096]{1,0:T(8,128)} %inn_h.1, f32[32,4,4096]{2,1,0:T(4,128)} %jac_h.1, s32[1,4096]{1,0:T(1,128)} %bitcast.15, s32[1,4096]{1,0:T(1,128)} %bitcast.16, s32[8,4096]{1,0:T(8,128)} %foot_h.1, f32[8,4096]{1,0:T(8,128)} %wgt_h.1), custom_call_target="tpu_custom_call" | custom-call | tf_op jit(solution)/shard_map/pack/pallas_call | solution.py:125
  9.3 104.2 %whole.1.x_ref = f32[10240,128]{1,0:T(8,128)} custom-call(f32[128,6,4,128]{3,2,1,0:T(4,128)} %bitcast.13, f32[32,256]{1,0:T(8,128)} %refs_1_.1, f32[32,256]{1,0:T(8,128)} %refs_2_.1, f32[10240,128]{1,0:T(8,128)} %bitcast.14, bf16[1536,384]{1,0:T(8,128)(2,1)} %constant.6.clone.refs_4_, bf16[1024,384]{1,0:T(8,128)(2,1)} %constant.7.clone.refs_5_, ...), custom_call_target="tpu_custom_call" | custom-call | tf_op jit(solution)/shard_map/whole/pallas_call | solution.py:512
  113.5 4.4 %placed.1 = f32[10240,128]{1,0:T(8,128)} custom-call(f32[10240,128]{1,0:T(8,128)} %whole.1.x_ref), custom_call_target="tpu_custom_call" | custom-call | tf_op jit(solution)/shard_map/placed/pallas_call | solution.py:553
